TPU v7x, 256 devices: a whole 4x4x8 slice. The times are simulated.
256 devices in a mesh: dom: 64 (over z, y, core), sub: 4 (over x).
Axes of the slice: x: 4, y: 4, z: 8, core: 2. Of those that a mesh axis runs over, the one named last changes fastest.
Arguments:
- adjoint_start: float32 [512, 384], P(('dom', 'sub')), may hold values from -6 to 6
- source: float32 [512, 384], P(('dom', 'sub')), may hold values from -6 to 6
- jac_off: bfloat16 [512, 5, 384, 384], P(('dom', 'sub')), may hold values from -0.125 to 0.125
- jac_diag: bfloat16 [512, 384, 384], P(('dom', 'sub')), may hold values from -0.11 to 3.11
- precond: bfloat16 [512, 384, 384], P(('dom', 'sub')), may hold values from -1 to 1
- surf_map: bfloat16 [384, 384], replicated, may hold values from -0.3125 to 0.3125
- neighbours: int32 [512, 5], P(('dom', 'sub')), may hold values from 0 to 511, as said below
- owner: int32 [512], P(('dom', 'sub')), may hold values from 0 to 255
- surface_grad: float32 [256, 384], P(('dom', 'sub')), may hold values from -6 to 6
Outputs:
- adjoint: float32 [512, 384], P(('dom', 'sub'))
- sensitivity: float32 [256, 384], P(('dom', 'sub'))
Inputs may be any that keep to these rules, and one draw needn't show every extreme that they name: `neighbours`: every device holds 2 consecutive block rows, devices taken dom-major. Slot 0 names a row of the same device; slots 1 and 2 name rows of the device one step higher and one step lower along dom, cyclically, with the same sub index; slots 3 and 4 likewise along sub.
All inputs are finite; a program needn't handle non-finite values.
Results may differ from a plain program's by a relative error of at most 0.0077.
Values may be sent and summed in bfloat16 or wider, within the bound.
No kernel may reach another device: no remote copies, remote signals or barrier semaphores. Data moves between devices by JAX's collectives and lax.ppermute only.
A program may use at most 64 MiB of HBM per device.

v0:
```python
import jax
import jax.numpy as jnp
from jax import lax
from jax.sharding import PartitionSpec as P

ITERS = 2


def shifted(block, axis, distance):
    devices = range(lax.axis_size(axis))
    route = [((i - distance) % len(devices), i) for i in devices]
    return lax.ppermute(block, axis, route)


def collect_slot(partials, targets, column):
    row_count = partials.shape[0]
    matches = targets[:, column][:, None] == jnp.arange(row_count, dtype=jnp.int32)[None, :]
    spread = jnp.where(matches[:, :, None], partials[:, column][:, None, :], jnp.float32(0.0))
    return jnp.sum(spread, axis=0)


def on_device(
    adjoint_start, source, jac_off, jac_diag, precond, surf_map, neighbours, owner, surface_grad
):
    row_count = adjoint_start.shape[0]
    targets = neighbours % row_count
    adjoint = adjoint_start
    for iteration in range(ITERS):
        adjoint_low = adjoint.astype(jnp.bfloat16)
        partials = jnp.einsum(
            "rb,rkbc->rkc", adjoint_low, jac_off, preferred_element_type=jnp.float32
        )
        own_term = jnp.einsum(
            "rb,rbc->rc", adjoint_low, jac_diag, preferred_element_type=jnp.float32
        )
        transposed = own_term + collect_slot(partials, targets, 0)
        transposed = transposed + shifted(collect_slot(partials, targets, 1), "dom", 1)
        transposed = transposed + shifted(collect_slot(partials, targets, 2), "dom", -1)
        transposed = transposed + shifted(collect_slot(partials, targets, 3), "sub", 1)
        transposed = transposed + shifted(collect_slot(partials, targets, 4), "sub", -1)
        residual = source - transposed
        residual_low = residual.astype(jnp.bfloat16)
        adjoint = adjoint + jnp.einsum(
            "rb,rbc->rc", residual_low, precond, preferred_element_type=jnp.float32
        )
    final_low = adjoint.astype(jnp.bfloat16)
    contribution = jnp.dot(final_low, surf_map, preferred_element_type=jnp.float32).astype(
        jnp.bfloat16
    )
    patch_count = surface_grad.shape[0]
    onehot = (
        owner[:, None]
        == jnp.arange(lax.axis_size(("dom", "sub")) * patch_count, dtype=jnp.int32)[None, :]
    ).astype(jnp.bfloat16)
    summed = lax.psum_scatter(
        jnp.dot(onehot.T, contribution, preferred_element_type=jnp.float32),
        ("dom", "sub"),
        scatter_dimension=0,
        tiled=True,
    )
    sensitivity = surface_grad - summed
    return (adjoint, sensitivity)


def solution(mesh):
    return jax.shard_map(
        on_device,
        mesh=mesh,
        in_specs=(
            P(("dom", "sub"), None),
            P(("dom", "sub"), None),
            P(("dom", "sub"), None, None, None),
            P(("dom", "sub"), None, None),
            P(("dom", "sub"), None, None),
            P(),
            P(("dom", "sub"), None),
            P(("dom", "sub")),
            P(("dom", "sub"), None),
        ),
        out_specs=(P(("dom", "sub"), None), P(("dom", "sub"), None)),
        check_vma=False,
    )
```

profile of v0, /device:TPU:1, one launch (start us, length us, event | category | flops | bytes accessed | tf_op | source)
XLA Modules:
  0.0 292.1 jit_solution(16636576329685305073)
XLA Ops:
  7.3 0.8 convert_bitcast_fusion.3
  8.1 1.3 copy-done
  9.4 0.5 fusion.20
  10.0 0.2 slice_reduce_fusion.4
  10.3 0.1 select_reduce_fusion.8
  10.3 2.7 collective-permute-start
  13.2 0.6 collective-permute-start.1
  13.9 0.7 collective-permute-start.2
  14.8 2.0 collective-permute-start.3
  16.9 0.2 fusion.22
  17.2 0.4 collective-permute-done.2
  17.7 0.2 fusion.18
  17.9 0.5 fusion.14
  18.5 2.8 collective-permute-start.4
  21.4 4.9 %collective-permute-start.5 = (f32[2,384]{1,0:T(2,128)S(1)}, f32[2,384]{1,0:T(2,128)S(1)}, u32[]{:S(2)}, u32[]{:S(2)}) collective-permute-start(f32[2,384]{1,0:T(2,128)S(1)} %select_reduce_fusion.2), channel_id=1, source_target_pairs={{4,0},{8,4},{12,8},{16,12},{20,16},{24,20},{28,24},{32,28},{36,32}... | collective-permute-start | bytes 9224 | tf_op jit(solution)/shard_map/ppermute | solution.py:12
  26.3 1.2 collective-permute-start.6
  27.6 1.5 collective-permute-start.7
  29.1 0.2 fusion.16
  29.4 0.6 collective-permute-done.6
  30.0 0.1 collective-permute-done.7
  30.1 0.2 fusion.12
  30.3 2.1 fusion
  32.4 251.6 %all-reduce.3.cloned.1.call-done = f32[256,384]{1,0:T(8,128)} async-done(((f32[256,384]{1,0:T(8,128)}), f32[256,384]{1,0:T(8,128)}) %all-reduce.3.cloned.1.call-update) | async-done | bytes 393232
  284.0 1.3 dynamic-slice_subtract_fusion
  (47 shorter events, 1.3 us)
Async XLA Ops:
  7.2 2.2 copy-start
  7.2 10.7 %copy-start.3 = (f32[2,384]{1,0:T(2,128)S(1)}, f32[2,384]{1,0:T(2,128)}, u32[]{:S(2)}) copy-start(f32[2,384]{1,0:T(2,128)} %param.9) | copy-start | bytes 9220
  7.2 2.8 copy-start.7
  7.2 9.7 %copy-start.1 = (bf16[2,384,384]{2,1,0:T(8,128)(2,1)S(1)}, bf16[2,384,384]{2,1,0:T(8,128)(2,1)}, u32[]{:S(2)}) copy-start(bf16[2,384,384]{2,1,0:T(8,128)(2,1)} %param.12) | copy-start | bytes 1769476
  7.2 10.4 %copy-start.5 = (f32[2,384]{1,0:T(2,128)S(1)}, f32[2,384]{1,0:T(2,128)}, u32[]{:S(2)}) copy-start(f32[2,384]{1,0:T(2,128)} %param.10) | copy-start | bytes 9220
  7.2 276.8 %all-reduce.3.cloned.1.call-start = ((), (), s32[]{:S(2)}) async-start(), calls=%async_computation | async-start | bytes 786432
  7.3 10.4 %copy-start.2 = (bf16[2,384,384]{2,1,0:T(8,128)(2,1)S(1)}, bf16[2,384,384]{2,1,0:T(8,128)(2,1)}, u32[]{:S(2)}) copy-start(bf16[2,384,384]{2,1,0:T(8,128)(2,1)} %param.13) | copy-start | bytes 1769476
  9.9 20.4 %copy-start.8 = (s32[2]{0:T(128)S(1)}, s32[2]{0:T(128)}, u32[]{:S(2)}) copy-start(s32[2]{0:T(128)} %param.16) | copy-start | bytes 28
  10.3 6.8 %collective-permute-start = (f32[2,384]{1,0:T(2,128)S(1)}, f32[2,384]{1,0:T(2,128)S(1)}, u32[]{:S(2)}, u32[]{:S(2)}) collective-permute-start(f32[2,384]{1,0:T(2,128)S(1)} %select_reduce_fusion.8), channel_id=1, source_target_pairs={{252,0},{0,4},{4,8},{8,12},{12,16},{16,20},{20,24},{24,28},{28,32}... | collective-permute-start | bytes 9224 | tf_op jit(solution)/shard_map/ppermute | solution.py:12
  13.2 4.0 %collective-permute-start.1 = (f32[2,384]{1,0:T(2,128)S(1)}, f32[2,384]{1,0:T(2,128)S(1)}, u32[]{:S(2)}, u32[]{:S(2)}) collective-permute-start(f32[2,384]{1,0:T(2,128)S(1)} %select_reduce_fusion.7), channel_id=1, source_target_pairs={{4,0},{8,4},{12,8},{16,12},{20,16},{24,20},{28,24},{32,28},{36,32}... | collective-permute-start | bytes 9224 | tf_op jit(solution)/shard_map/ppermute | solution.py:12
  13.9 3.7 %collective-permute-start.2 = (f32[2,384]{1,0:T(2,128)S(1)}, f32[2,384]{1,0:T(2,128)S(1)}, u32[]{:S(2)}, u32[]{:S(2)}) collective-permute-start(f32[2,384]{1,0:T(2,128)S(1)} %select_reduce_fusion.6), channel_id=1, source_target_pairs={{3,0},{0,1},{1,2},{2,3},{7,4},{4,5},{5,6},{6,7},{11,8},{8,9},{9,10... | collective-permute-start | bytes 9224 | tf_op jit(solution)/shard_map/ppermute | solution.py:12
  14.8 2.8 collective-permute-start.3
  17.6 266.4 %copy-start.6 = (f32[1,384]{1,0:T(1,128)S(1)}, f32[1,384]{1,0:T(1,128)}, u32[]{:S(2)}) copy-start(f32[1,384]{1,0:T(1,128)} %param.17) | copy-start | bytes 4612
  18.5 10.9 %collective-permute-start.4 = (f32[2,384]{1,0:T(2,128)S(1)}, f32[2,384]{1,0:T(2,128)S(1)}, u32[]{:S(2)}, u32[]{:S(2)}) collective-permute-start(f32[2,384]{1,0:T(2,128)S(1)} %select_reduce_fusion.3), channel_id=1, source_target_pairs={{252,0},{0,4},{4,8},{8,12},{12,16},{16,20},{20,24},{24,28},{28,32}... | collective-permute-start | bytes 9224 | tf_op jit(solution)/shard_map/ppermute | solution.py:12
  21.4 8.0 %collective-permute-start.5 = (f32[2,384]{1,0:T(2,128)S(1)}, f32[2,384]{1,0:T(2,128)S(1)}, u32[]{:S(2)}, u32[]{:S(2)}) collective-permute-start(f32[2,384]{1,0:T(2,128)S(1)} %select_reduce_fusion.2), channel_id=1, source_target_pairs={{4,0},{8,4},{12,8},{16,12},{20,16},{24,20},{28,24},{32,28},{36,32}... | collective-permute-start | bytes 9224 | tf_op jit(solution)/shard_map/ppermute | solution.py:12
  26.3 3.7 %collective-permute-start.6 = (f32[2,384]{1,0:T(2,128)S(1)}, f32[2,384]{1,0:T(2,128)S(1)}, u32[]{:S(2)}, u32[]{:S(2)}) collective-permute-start(f32[2,384]{1,0:T(2,128)S(1)} %select_reduce_fusion.1), channel_id=1, source_target_pairs={{3,0},{0,1},{1,2},{2,3},{7,4},{4,5},{5,6},{6,7},{11,8},{8,9},{9,10... | collective-permute-start | bytes 9224 | tf_op jit(solution)/shard_map/ppermute | solution.py:12
  27.6 2.5 collective-permute-start.7
  30.3 255.0 %copy-start.4 = (f32[2,384]{1,0:T(2,128)}, f32[2,384]{1,0:T(2,128)S(1)}, u32[]{:S(2)}) copy-start(f32[2,384]{1,0:T(2,128)S(1)} %bitcast_add_fusion) | copy-start | bytes 9220
Sparse Core Ops, SparseCore 0:
  32.5 251.4 all-reduce.2
where the time goes:
time: 292 us
  waiting for transfers between devices  253 us (87%)
  starting transfers between devices  16.4 us (6%)
  between operations  14.2 us (5%)
  matrix products  3.83 us (1%)
  other arithmetic  3.35 us (1%)
    unnamed x2, waiting for transfers between devices  252 us
    ppermute x8, starting transfers between devices, shifted(): return lax.ppermute(block, axis, route)  16.3 us
  transfers between devices with their start and end apart: 9, of which 4 were waited for; matrix products, arithmetic and copies ran while one was open for 0% of the time, Pallas kernels for 0%

commit v1 on v0

v1 whole, which is shorter than its diff:
```python
import jax
import jax.numpy as jnp
from jax import lax
from jax.sharding import Mesh, PartitionSpec as P

ITERS = 2
CUT = {"z": 8, "y": 4, "core": 2, "x": 4}
ALL = tuple(CUT)


def pairs(axis, first):
    subs = CUT["x"]
    devices = CUT["z"] * CUT["y"] * CUT["core"] * subs
    route = []
    for device in range(devices):
        dom, sub = divmod(device, subs)
        if axis == "dom":
            doms = devices // subs
            dom = (((dom - first) % doms ^ 1) + first) % doms
        else:
            sub = (((sub - first) % subs ^ 1) + first) % subs
        route.append((device, dom * subs + sub))
    return route


def collect(partials, rows, column):
    matches = rows[:, column][:, None] == jnp.arange(partials.shape[0], dtype=jnp.int32)[None, :]
    spread = jnp.where(matches[:, :, None], partials[:, column][:, None, :], jnp.float32(0.0))
    return jnp.sum(spread, axis=0)


def on_device(
    adjoint_start, source, jac_off, jac_diag, precond, surf_map, neighbours, owner, surface_grad
):
    row_count, width = adjoint_start.shape
    rows = neighbours % row_count
    even_dom = lax.axis_index("core") == 0
    even_sub = lax.axis_index("x") % 2 == 0
    adjoint = adjoint_start
    for _ in range(ITERS):
        adjoint_low = adjoint.astype(jnp.bfloat16)
        partials = jnp.einsum(
            "rb,rkbc->rkc", adjoint_low, jac_off, preferred_element_type=jnp.float32
        )
        up_dom, down_dom, up_sub, down_sub = (collect(partials, rows, k) for k in range(1, 5))
        came = [
            lax.ppermute(jnp.where(even_dom, up_dom, down_dom), ALL, pairs("dom", 0)),
            lax.ppermute(jnp.where(even_sub, up_sub, down_sub), ALL, pairs("sub", 0)),
            lax.ppermute(jnp.where(even_sub, down_sub, up_sub), ALL, pairs("sub", 1)),
            lax.ppermute(jnp.where(even_dom, down_dom, up_dom), ALL, pairs("dom", 1)),
        ]
        own_term = jnp.einsum(
            "rb,rbc->rc", adjoint_low, jac_diag, preferred_element_type=jnp.float32
        )
        transposed = own_term + collect(partials, rows, 0)
        for part in came:
            transposed = transposed + part
        residual_low = (source - transposed).astype(jnp.bfloat16)
        adjoint = adjoint + jnp.einsum(
            "rb,rbc->rc", residual_low, precond, preferred_element_type=jnp.float32
        )
    final_low = adjoint.astype(jnp.bfloat16)
    contribution = jnp.dot(final_low, surf_map, preferred_element_type=jnp.float32).astype(
        jnp.bfloat16
    )
    plane = CUT["y"] * CUT["x"]
    tagged = jnp.concatenate(
        [contribution, jnp.broadcast_to(owner.astype(jnp.bfloat16)[:, None], (row_count, 128))],
        axis=1,
    )
    got = lax.all_to_all(
        jnp.broadcast_to(tagged[None], (plane, row_count, width + 128)),
        ("y", "x"), 0, 0, tiled=True,
    ).reshape(plane * row_count, width + 128)
    owners = got[:, width].astype(jnp.int32)
    line = CUT["z"] * CUT["core"]
    place = jnp.arange(line, dtype=jnp.int32)
    z, core = place // CUT["core"], place % CUT["core"]
    patch = ((z * CUT["y"] + lax.axis_index("y")) * CUT["core"] + core) * CUT["x"] + lax.axis_index("x")
    onehot = (patch[:, None] == owners[None, :]).astype(jnp.bfloat16)
    sums = jnp.dot(onehot, got[:, :width], preferred_element_type=jnp.float32)
    parts = lax.all_to_all(sums, ("z", "core"), 0, 0, tiled=True)
    sensitivity = surface_grad - jnp.sum(parts, axis=0, keepdims=True)
    return (adjoint, sensitivity)


def solution(mesh):
    cut = Mesh(mesh.devices.reshape(tuple(CUT.values())), ALL)
    return jax.shard_map(
        on_device,
        mesh=cut,
        in_specs=(
            P(ALL, None),
            P(ALL, None),
            P(ALL, None, None, None),
            P(ALL, None, None),
            P(ALL, None, None),
            P(),
            P(ALL, None),
            P(ALL),
            P(ALL, None),
        ),
        out_specs=(P(ALL, None), P(ALL, None)),
        check_vma=False,
    )
```

time: 292 us -> 60.1 us (0.21)
  waiting for transfers between devices: 253 us -> 8.16 us
  blocking collectives: 0 us -> 14.3 us
  between operations: 14.2 us -> 0.87 us
  other arithmetic: 3.35 us -> 11.3 us
    unnamed x2 -> x0, waiting for transfers between devices: 252 us -> none
    all_to_all x0 -> x1, blocking collectives: none -> 14.3 us  [on_device(): parts = lax.all_to_all(sums, ('z', 'core'), 0, 0, tiled=True)]
    all_to_all x0 -> x1, waiting for transfers between devices: none -> 6.37 us  [on_device(): lax.all_to_all(jnp.broadcast_to(tagged[None], (plane, row_count, width +...]
    all_to_all x0 -> x1, starting transfers between devices: none -> 3.5 us  [on_device(): lax.all_to_all(jnp.broadcast_to(tagged[None], (plane, row_count, width +...]
  transfers between devices with their start and end apart: 9 -> 9, of which waited for: 4 -> 3; matrix products, arithmetic and copies ran while one was open for 0% -> 8% of each run, Pallas kernels for 0% -> 0%
where the time goes in v1:
time: 60.1 us; the launch traced here: 59.7 us
  starting transfers between devices  19.3 us (32%)
  blocking collectives  14.3 us (24%)
  other arithmetic  11.3 us (19%)
  waiting for transfers between devices  8.16 us (14%)
  matrix products  3.17 us (5%)
  local copies, waits for them, and re-layouts  2.58 us (4%)
  between operations  0.87 us (1%)
    all_to_all x1, blocking collectives, on_device(): parts = lax.all_to_all(sums, ('z', 'core'), 0, 0, tiled=True)  14.3 us
    ppermute x2, starting transfers between devices, on_device(): lax.ppermute(jnp.where(even_dom, up_dom, down_dom), ALL, pairs('dom', 0))  11.3 us
    all_to_all x1, waiting for transfers between devices, on_device(): lax.all_to_all(jnp.broadcast_to(tagged[None], (plane, row_count, width +...  6.37 us
    ppermute x2, starting transfers between devices, on_device(): lax.ppermute(jnp.where(even_sub, down_sub, up_sub), ALL, pairs('sub', 1))  3.61 us
    reduce_sum x10, other arithmetic, collect(): return jnp.sum(spread, axis=0)  3.51 us
    all_to_all x1, starting transfers between devices, on_device(): lax.all_to_all(jnp.broadcast_to(tagged[None], (plane, row_count, width +...  3.5 us
    eq x3, other arithmetic, collect(): rows[:, column][:, None]  2.15 us
    dot_general x2, matrix products, on_device(): jnp.einsum('rb,rbc->rc', residual_low, precond, preferred_element_type=jn...  1.45 us
  transfers between devices with their start and end apart: 9, of which 3 were waited for; matrix products, arithmetic and copies ran while one was open for 8% of the time, Pallas kernels for 0%

profile of v1, /device:TPU:1, one launch (start us, length us, event | category | flops | bytes accessed | tf_op | source)
XLA Modules:
  0.0 59.7 jit_solution(16456794618156866640)
XLA Ops:
  0.7 0.8 %and_select_fusion.2 = s32[2,5]{1,0:T(2,128)S(1)} fusion(s32[2,5]{1,0:T(2,128)} %param.15), kind=kLoop, calls=%fused_computation.70 | loop fusion | flops 110 | bytes 80 | tf_op jit(solution)/shard_map/jit(remainder)/select_n | solution.py:36
  1.5 0.8 %slice_reduce_fusion.4 = (s32[2]{0:T(128)}, s32[2]{0:T(128)}, s32[2]{0:T(128)}, s32[2]{0:T(128)}, s32[2]{0:T(128)}) fusion(s32[2,5]{1,0:T(2,128)S(1)} %and_select_fusion.2), kind=kLoop, calls=%fused_computation.88 | loop fusion | bytes 80 | tf_op jit(solution)/shard_map/slice | solution.py:27
  2.3 0.7 %convert_bitcast_fusion.3 = (bf16[2,384,1]{1,0,2:T(2,128)(2,1)S(1)}, bf16[2,384,1,1]{1,0,2,3:T(2,128)(2,1)S(1)}) fusion(f32[2,384]{1,0:T(2,128)} %param.9), kind=kLoop, calls=%fused_computation.92 | loop fusion | flops 768 | bytes 6144 | tf_op jit(solution)/shard_map/convert_element_type | solution.py:41
  4.1 0.7 %iota_compare_fusion.2 = (pred[2,2]{1,0:T(4,128)(4,1)S(1)}, pred[2,2]{1,0:T(4,128)(4,1)S(1)}) fusion(s32[2]{0:T(128)} %get-tuple-element.5, s32[2]{0:T(128)} %get-tuple-element.6), kind=kLoop, calls=%fused_computation.83 | loop fusion | flops 8 | bytes 24 | tf_op jit(solution)/shard_map/eq | solution.py:27
  4.9 0.8 %select_reduce_fusion.7 = f32[2,384]{1,0:T(2,128)S(1)} fusion(pred[2,2]{1,0:T(4,128)(4,1)S(1)} %get-tuple-element.31, f32[2,384]{1,0:T(2,128)} %get-tuple-element.15), kind=kLoop, calls=%fused_computation.14 | loop fusion | flops 2304 | bytes 6148 | tf_op jit(solution)/shard_map/reduce_sum | solution.py:29
  5.6 0.7 %select_reduce_fusion.8 = f32[2,384]{1,0:T(2,128)S(1)} fusion(pred[2,2]{1,0:T(4,128)(4,1)S(1)} %get-tuple-element.32, f32[2,384]{1,0:T(2,128)} %get-tuple-element.16), kind=kLoop, calls=%fused_computation.15 | loop fusion | flops 2304 | bytes 6148 | tf_op jit(solution)/shard_map/reduce_sum | solution.py:29
  7.0 3.2 %collective-permute-start = (f32[2,384]{1,0:T(2,128)}, f32[2,384]{1,0:T(2,128)}, u32[]{:S(2)}, u32[]{:S(2)}) collective-permute-start(f32[2,384]{1,0:T(2,128)} %get-tuple-element.23), channel_id=1, source_target_pairs={{0,4},{1,5},{2,6},{3,7},{4,0},{5,1},{6,2},{7,3},{8,12},{9,13},{10,... | collective-permute-start | bytes 9224 | tf_op jit(solution)/shard_map/ppermute | solution.py:47
  10.2 0.7 %iota_compare_fusion = (pred[2,2]{1,0:T(4,128)(4,1)S(1)}, pred[2,2]{1,0:T(4,128)(4,1)S(1)}) fusion(s32[2]{0:T(128)} %get-tuple-element.3, s32[2]{0:T(128)} %get-tuple-element.4), kind=kLoop, calls=%fused_computation.79 | loop fusion | flops 8 | bytes 24 | tf_op jit(solution)/shard_map/eq | solution.py:27
  10.9 0.8 %select_reduce_fusion.5 = f32[2,384]{1,0:T(2,128)S(1)} fusion(pred[2,2]{1,0:T(4,128)(4,1)S(1)} %get-tuple-element.29, f32[2,384]{1,0:T(2,128)} %get-tuple-element.13), kind=kLoop, calls=%fused_computation.12 | loop fusion | flops 2304 | bytes 6148 | tf_op jit(solution)/shard_map/reduce_sum | solution.py:29
  12.4 0.7 %collective-permute-start.1 = (f32[2,384]{1,0:T(2,128)}, f32[2,384]{1,0:T(2,128)}, u32[]{:S(2)}, u32[]{:S(2)}) collective-permute-start(f32[2,384]{1,0:T(2,128)} %get-tuple-element.25), channel_id=1, source_target_pairs={{0,1},{1,0},{2,3},{3,2},{4,5},{5,4},{6,7},{7,6},{8,9},{9,8},{10,11... | collective-permute-start | bytes 9224 | tf_op jit(solution)/shard_map/ppermute | solution.py:48
  13.0 1.8 %collective-permute-start.2 = (f32[2,384]{1,0:T(2,128)}, f32[2,384]{1,0:T(2,128)}, u32[]{:S(2)}, u32[]{:S(2)}) collective-permute-start(f32[2,384]{1,0:T(2,128)} %get-tuple-element.26), channel_id=1, source_target_pairs={{0,3},{1,2},{2,1},{3,0},{4,7},{5,6},{6,5},{7,4},{8,11},{9,10},{10,... | collective-permute-start | bytes 9224 | tf_op jit(solution)/shard_map/ppermute | solution.py:49
  14.8 0.7 %iota_compare_fusion.4 = pred[2,2]{1,0:T(4,128)(4,1)S(1)} fusion(s32[2]{0:T(128)} %get-tuple-element.2), kind=kLoop, calls=%fused_computation.87 | loop fusion | flops 4 | bytes 12 | tf_op jit(solution)/shard_map/eq | solution.py:27
  16.1 0.8 %select_reduce_fusion.9 = f32[2,384]{1,0:T(2,128)S(1)} fusion(pred[2,2]{1,0:T(4,128)(4,1)S(1)} %iota_compare_fusion.4, f32[2,384]{1,0:T(2,128)} %get-tuple-element.12), kind=kLoop, calls=%fused_computation.16 | loop fusion | flops 2304 | bytes 6148 | tf_op jit(solution)/shard_map/reduce_sum | solution.py:29
  16.9 0.7 %convert_element_type.38 = bf16[2]{0:T(256)(128)(2,1)S(1)} convert(s32[2]{0:T(128)} %param.16) | non-fusion elementwise | flops 2 | bytes 12 | tf_op jit(solution)/shard_map/convert_element_type | solution.py:68
  17.7 0.7 %fusion.30 = bf16[2,384,1]{1,0,2:T(2,128)(2,1)S(1)} fusion(f32[2,384]{1,0:T(2,128)S(1)} %copy-done.6, f32[2,384]{1,0:T(2,128)} %collective-permute-done.3, f32[2,384]{1,0:T(2,128)} %collective-permute-done.2, f32[2,384]{1,0:T(2,128)} %collective-permute-done.1, f32[2,384]{1,0:T(2,128)} %collective-permute-done, f32[2,384]{1,0:T(2,128)S(1)} %select_reduce_fusion.9, ...), kind=kLoop, calls=%fused_computation.74 | loop fusion | flops 5376 | bytes 23040 | tf_op jit(solution)/shard_map/convert_element_type | solution.py:58
  18.4 1.3 %fusion.20 = f32[2,1,384]{2,1,0:T(1,128)S(1)} fusion(bf16[2,384,384]{2,1,0:T(8,128)(2,1)} %param.13, bf16[2,384,1]{1,0,2:T(2,128)(2,1)S(1)} %fusion.30), kind=kOutput, calls=%fused_computation.49 | convolution fusion | flops 589824 | bytes 594432 | tf_op jit(solution)/shard_map/rb,rbc->rc/dot_general | solution.py:59
  20.8 8.1 %collective-permute-start.4 = (f32[2,384]{1,0:T(2,128)S(1)}, f32[2,384]{1,0:T(2,128)S(1)}, u32[]{:S(2)}, u32[]{:S(2)}) collective-permute-start(f32[2,384]{1,0:T(2,128)S(1)} %get-tuple-element.19), channel_id=1, source_target_pairs={{0,4},{1,5},{2,6},{3,7},{4,0},{5,1},{6,2},{7,3},{8,12},{9,13},{10,... | collective-permute-start | bytes 9224 | tf_op jit(solution)/shard_map/ppermute | solution.py:47
  29.1 1.8 %collective-permute-start.6 = (f32[2,384]{1,0:T(2,128)S(1)}, f32[2,384]{1,0:T(2,128)S(1)}, u32[]{:S(2)}, u32[]{:S(2)}) collective-permute-start(f32[2,384]{1,0:T(2,128)S(1)} %get-tuple-element.22), channel_id=1, source_target_pairs={{0,3},{1,2},{2,1},{3,0},{4,7},{5,6},{6,5},{7,4},{8,11},{9,10},{10,... | collective-permute-start | bytes 9224 | tf_op jit(solution)/shard_map/ppermute | solution.py:49
  30.9 0.9 %collective-permute-done.7 = f32[2,384]{1,0:T(2,128)S(1)} collective-permute-done((f32[2,384]{1,0:T(2,128)S(1)}, f32[2,384]{1,0:T(2,128)S(1)}, u32[]{:S(2)}, u32[]{:S(2)}) %collective-permute-start.7) | collective-permute-done | bytes 3104 | tf_op jit(solution)/shard_map/ppermute | solution.py:50
  31.9 0.9 %collective-permute-done.6 = f32[2,384]{1,0:T(2,128)S(1)} collective-permute-done((f32[2,384]{1,0:T(2,128)S(1)}, f32[2,384]{1,0:T(2,128)S(1)}, u32[]{:S(2)}, u32[]{:S(2)}) %collective-permute-start.6) | collective-permute-done | bytes 3104 | tf_op jit(solution)/shard_map/ppermute | solution.py:49
  33.8 3.5 %all-to-all-start = ((bf16[16,2,512]{2,1,0:T(2,128)(2,1)}), bf16[16,2,512]{2,1,0:T(2,128)(2,1)S(1)}, u32[]{:S(2)}, u32[]{:S(2)}) async-start(bf16[16,2,512]{2,1,0:T(2,128)(2,1)} %broadcast_in_dim.193), calls=%async_computation | async-start | bytes 65536 | tf_op jit(solution)/shard_map/all_to_all | solution.py:71
  37.4 6.4 %all-to-all-done = bf16[16,2,512]{2,1,0:T(2,128)(2,1)S(1)} async-done(((bf16[16,2,512]{2,1,0:T(2,128)(2,1)}), bf16[16,2,512]{2,1,0:T(2,128)(2,1)S(1)}, u32[]{:S(2)}, u32[]{:S(2)}) %all-to-all-start) | async-done | bytes 32800 | tf_op jit(solution)/shard_map/all_to_all | solution.py:71
  44.1 14.3 %all_to_all.14 = f32[16,1,384]{2,1,0:T(1,128)S(1)} all-to-all(f32[16,1,384]{2,1,0:T(1,128)S(1)} %copy.13), channel_id=1, replica_groups=mesh['z'=8,'y'=4,'core'=2,'x'=4] {'z','core'}, dimensions={0} | all-to-all | bytes 49152 | tf_op jit(solution)/shard_map/all_to_all | solution.py:82
  58.4 1.2 %reshape_subtract_fusion = f32[1,384]{1,0:T(1,128)} fusion(f32[1,384]{1,0:T(1,128)} %param.17, f32[384]{0:T(512)S(1)} %reduce_sum.109), kind=kLoop, calls=%fused_computation.71 | loop fusion | flops 384 | bytes 4608 | tf_op jit(solution)/shard_map/sub | solution.py:83
  (75 shorter events, 5.8 us)
Async XLA Ops:
  0.6 2.4 %copy-start = (bf16[2,5,384,384]{3,2,1,0:T(8,128)(2,1)S(1)}, bf16[2,5,384,384]{3,2,1,0:T(8,128)(2,1)}, u32[]{:S(2)}) copy-start(bf16[2,5,384,384]{3,2,1,0:T(8,128)(2,1)} %param.11) | copy-start | bytes 8847364
  0.6 19.0 %copy-start.4 = (f32[2,384]{1,0:T(2,128)S(1)}, f32[2,384]{1,0:T(2,128)}, u32[]{:S(2)}) copy-start(f32[2,384]{1,0:T(2,128)} %param.9) | copy-start | bytes 9220
  0.7 14.9 %copy-start.1 = (bf16[2,384,384]{2,1,0:T(8,128)(2,1)S(1)}, bf16[2,384,384]{2,1,0:T(8,128)(2,1)}, u32[]{:S(2)}) copy-start(bf16[2,384,384]{2,1,0:T(8,128)(2,1)} %param.12) | copy-start | bytes 1769476
  0.7 17.0 %copy-start.6 = (f32[2,384]{1,0:T(2,128)S(1)}, f32[2,384]{1,0:T(2,128)}, u32[]{:S(2)}) copy-start(f32[2,384]{1,0:T(2,128)} %param.10) | copy-start | bytes 9220
  4.9 2.1 %copy-start.7 = (pred[2,2]{1,0:T(4,128)(4,1)}, pred[2,2]{1,0:T(4,128)(4,1)S(1)}, u32[]{:S(2)}) copy-start(pred[2,2]{1,0:T(4,128)(4,1)S(1)} %get-tuple-element.32) | copy-start | bytes 16
  7.0 10.7 %collective-permute-start = (f32[2,384]{1,0:T(2,128)}, f32[2,384]{1,0:T(2,128)}, u32[]{:S(2)}, u32[]{:S(2)}) collective-permute-start(f32[2,384]{1,0:T(2,128)} %get-tuple-element.23), channel_id=1, source_target_pairs={{0,4},{1,5},{2,6},{3,7},{4,0},{5,1},{6,2},{7,3},{8,12},{9,13},{10,... | collective-permute-start | bytes 9224 | tf_op jit(solution)/shard_map/ppermute | solution.py:47
  10.2 7.4 %collective-permute-start.3 = (f32[2,384]{1,0:T(2,128)}, f32[2,384]{1,0:T(2,128)}, u32[]{:S(2)}, u32[]{:S(2)}) collective-permute-start(f32[2,384]{1,0:T(2,128)} %get-tuple-element.24), channel_id=1, source_target_pairs={{0,252},{1,253},{2,254},{3,255},{4,8},{5,9},{6,10},{7,11},{8,4},{9... | collective-permute-start | bytes 9224 | tf_op jit(solution)/shard_map/ppermute | solution.py:50
  10.9 0.8 %copy-start.13 = (pred[2,2]{1,0:T(4,128)(4,1)}, pred[2,2]{1,0:T(4,128)(4,1)S(1)}, u32[]{:S(2)}) copy-start(pred[2,2]{1,0:T(4,128)(4,1)S(1)} %get-tuple-element.29) | copy-start | bytes 16
  10.9 4.9 %copy-start.11 = (pred[2,2]{1,0:T(4,128)(4,1)}, pred[2,2]{1,0:T(4,128)(4,1)S(1)}, u32[]{:S(2)}) copy-start(pred[2,2]{1,0:T(4,128)(4,1)S(1)} %get-tuple-element.30) | copy-start | bytes 16
  12.4 5.3 %collective-permute-start.1 = (f32[2,384]{1,0:T(2,128)}, f32[2,384]{1,0:T(2,128)}, u32[]{:S(2)}, u32[]{:S(2)}) collective-permute-start(f32[2,384]{1,0:T(2,128)} %get-tuple-element.25), channel_id=1, source_target_pairs={{0,1},{1,0},{2,3},{3,2},{4,5},{5,4},{6,7},{7,6},{8,9},{9,8},{10,11... | collective-permute-start | bytes 9224 | tf_op jit(solution)/shard_map/ppermute | solution.py:48
  13.0 4.6 %collective-permute-start.2 = (f32[2,384]{1,0:T(2,128)}, f32[2,384]{1,0:T(2,128)}, u32[]{:S(2)}, u32[]{:S(2)}) collective-permute-start(f32[2,384]{1,0:T(2,128)} %get-tuple-element.26), channel_id=1, source_target_pairs={{0,3},{1,2},{2,1},{3,0},{4,7},{5,6},{6,5},{7,4},{8,11},{9,10},{10,... | collective-permute-start | bytes 9224 | tf_op jit(solution)/shard_map/ppermute | solution.py:49
  16.8 3.6 %copy-start.14 = (pred[2,2]{1,0:T(4,128)(4,1)S(1)}, pred[2,2]{1,0:T(4,128)(4,1)}, u32[]{:S(2)}) copy-start(pred[2,2]{1,0:T(4,128)(4,1)} %copy-done.13) | copy-start | bytes 16
  16.8 3.7 %copy-start.12 = (pred[2,2]{1,0:T(4,128)(4,1)S(1)}, pred[2,2]{1,0:T(4,128)(4,1)}, u32[]{:S(2)}) copy-start(pred[2,2]{1,0:T(4,128)(4,1)} %copy-done.11) | copy-start | bytes 16
  16.9 3.7 %copy-start.10 = (pred[2,2]{1,0:T(4,128)(4,1)S(1)}, pred[2,2]{1,0:T(4,128)(4,1)}, u32[]{:S(2)}) copy-start(pred[2,2]{1,0:T(4,128)(4,1)} %copy-done.9) | copy-start | bytes 16
  16.9 3.8 %copy-start.8 = (pred[2,2]{1,0:T(4,128)(4,1)S(1)}, pred[2,2]{1,0:T(4,128)(4,1)}, u32[]{:S(2)}) copy-start(pred[2,2]{1,0:T(4,128)(4,1)} %copy-done.7) | copy-start | bytes 16
  16.9 14.0 %copy-start.16 = (pred[2,2]{1,0:T(4,128)(4,1)S(1)}, pred[2,2]{1,0:T(4,128)(4,1)}, u32[]{:S(2)}) copy-start(pred[2,2]{1,0:T(4,128)(4,1)} %copy-done.15) | copy-start | bytes 16
  16.9 15.8 %copy-start.2 = (bf16[2,384,384]{2,1,0:T(8,128)(2,1)S(1)}, bf16[2,384,384]{2,1,0:T(8,128)(2,1)}, u32[]{:S(2)}) copy-start(bf16[2,384,384]{2,1,0:T(8,128)(2,1)} %param.13) | copy-start | bytes 1769476
  16.9 16.0 %copy-start.3 = (bf16[384,384]{1,0:T(8,128)(2,1)S(1)}, bf16[384,384]{1,0:T(8,128)(2,1)}, u32[]{:S(2)}) copy-start(bf16[384,384]{1,0:T(8,128)(2,1)} %param.14) | copy-start | bytes 884740
  20.8 10.2 %collective-permute-start.4 = (f32[2,384]{1,0:T(2,128)S(1)}, f32[2,384]{1,0:T(2,128)S(1)}, u32[]{:S(2)}, u32[]{:S(2)}) collective-permute-start(f32[2,384]{1,0:T(2,128)S(1)} %get-tuple-element.19), channel_id=1, source_target_pairs={{0,4},{1,5},{2,6},{3,7},{4,0},{5,1},{6,2},{7,3},{8,12},{9,13},{10,... | collective-permute-start | bytes 9224 | tf_op jit(solution)/shard_map/ppermute | solution.py:47
  28.8 3.0 %collective-permute-start.7 = (f32[2,384]{1,0:T(2,128)S(1)}, f32[2,384]{1,0:T(2,128)S(1)}, u32[]{:S(2)}, u32[]{:S(2)}) collective-permute-start(f32[2,384]{1,0:T(2,128)S(1)} %get-tuple-element.20), channel_id=1, source_target_pairs={{0,252},{1,253},{2,254},{3,255},{4,8},{5,9},{6,10},{7,11},{8,4},{9... | collective-permute-start | bytes 9224 | tf_op jit(solution)/shard_map/ppermute | solution.py:50
  28.8 3.0 %collective-permute-start.5 = (f32[2,384]{1,0:T(2,128)S(1)}, f32[2,384]{1,0:T(2,128)S(1)}, u32[]{:S(2)}, u32[]{:S(2)}) collective-permute-start(f32[2,384]{1,0:T(2,128)S(1)} %get-tuple-element.21), channel_id=1, source_target_pairs={{0,1},{1,0},{2,3},{3,2},{4,5},{5,4},{6,7},{7,6},{8,9},{9,8},{10,11... | collective-permute-start | bytes 9224 | tf_op jit(solution)/shard_map/ppermute | solution.py:48
  29.1 3.7 %collective-permute-start.6 = (f32[2,384]{1,0:T(2,128)S(1)}, f32[2,384]{1,0:T(2,128)S(1)}, u32[]{:S(2)}, u32[]{:S(2)}) collective-permute-start(f32[2,384]{1,0:T(2,128)S(1)} %get-tuple-element.22), channel_id=1, source_target_pairs={{0,3},{1,2},{2,1},{3,0},{4,7},{5,6},{6,5},{7,4},{8,11},{9,10},{10,... | collective-permute-start | bytes 9224 | tf_op jit(solution)/shard_map/ppermute | solution.py:49
  33.0 26.7 %copy-start.5 = (f32[2,384]{1,0:T(2,128)}, f32[2,384]{1,0:T(2,128)S(1)}, u32[]{:S(2)}) copy-start(f32[2,384]{1,0:T(2,128)S(1)} %bitcast_add_fusion) | copy-start | bytes 9220
  33.8 9.9 %all-to-all-start = ((bf16[16,2,512]{2,1,0:T(2,128)(2,1)}), bf16[16,2,512]{2,1,0:T(2,128)(2,1)S(1)}, u32[]{:S(2)}, u32[]{:S(2)}) async-start(bf16[16,2,512]{2,1,0:T(2,128)(2,1)} %broadcast_in_dim.193), calls=%async_computation | async-start | bytes 65536 | tf_op jit(solution)/shard_map/all_to_all | solution.py:71
  (2 other events, 1.3 us)

commit v2 on v1

v2 whole, which is shorter than its diff:
```python
import jax
import jax.numpy as jnp
from jax import lax
from jax.experimental import pallas as pl
from jax.experimental.pallas import tpu as pltpu
from jax.sharding import Mesh, PartitionSpec as P

CUT = {"z": 8, "y": 4, "core": 2, "x": 4}
ALL = tuple(CUT)
LANES = 128
F32 = jnp.float32
BF16 = jnp.bfloat16
VMEM = pl.BlockSpec(memory_space=pltpu.VMEM)
SMEM = pl.BlockSpec(memory_space=pltpu.SMEM)
HBM = pl.BlockSpec(memory_space=pltpu.HBM)


def pairs(axis, first):
    subs = CUT["x"]
    devices = CUT["z"] * CUT["y"] * CUT["core"] * subs
    route = []
    for device in range(devices):
        dom, sub = divmod(device, subs)
        if axis == "dom":
            doms = devices // subs
            dom = (((dom - first) % doms ^ 1) + first) % doms
        else:
            sub = (((sub - first) % subs ^ 1) + first) % subs
        route.append((device, dom * subs + sub))
    return route


def placed(values, row, target):
    rows = lax.broadcasted_iota(jnp.int32, (8, values.shape[1]), 0)
    return jnp.where(rows == target, values[row : row + 1, :], 0.0).astype(BF16)


def matmul(left, right):
    return jnp.dot(left, right, preferred_element_type=F32)


def message_slots():
    core, odd = lax.axis_index("core"), lax.axis_index("x") % 2
    return 1 + core, 3 + odd, 4 - odd, 2 - core


def message(values, names_ref, slot, off_ref):
    count = values.shape[0]
    total = None
    for row in range(count):
        part = matmul(placed(values, row, names_ref[row, slot] % count), off_ref[row])
        total = part if total is None else total + part
    return total[:count]


def step(adjoint, source, local, came, precond_ref):
    residual = source - local
    for part in came:
        residual = residual - part[...]
    for row in range(adjoint.shape[0]):
        adjoint = adjoint + matmul(placed(residual, row, row), precond_ref[row])[: adjoint.shape[0]]
    return adjoint


def first_kernel(names_in, adjoint_in, off_in, c0, c1, c2, c3, names, adjoint, off, sems):
    slots = message_slots()
    copies = [
        pltpu.make_async_copy(off_in.at[:, slot], off.at[m], sems.at[m])
        for m, slot in enumerate(slots)
    ]
    heads = [
        pltpu.make_async_copy(names_in, names, sems.at[len(slots)]),
        pltpu.make_async_copy(adjoint_in, adjoint, sems.at[len(slots) + 1]),
    ]
    for copy in heads + copies:
        copy.start()
    for copy in heads:
        copy.wait()
    for m, (slot, out) in enumerate(zip(slots, (c0, c1, c2, c3), strict=True)):
        copies[m].wait()
        out[...] = message(adjoint[...], names, slot, off.at[m])


def local_kernel(names, adjoint, off, diag, out):
    values = adjoint[...]
    count = values.shape[0]
    total = None
    for row in range(values.shape[0]):
        part = matmul(placed(values, row, names[row, 0] % count), off[row, 0])
        part = part + matmul(placed(values, row, row), diag[row])
        total = part if total is None else total + part
    out[...] = total[: values.shape[0]]


def middle_kernel(names, adjoint, source, local, c0, c1, c2, c3, precond, off, new, *outs):
    values = step(adjoint[...], source[...], local[...], (c0, c1, c2, c3), precond)
    new[...] = values
    for slot, out in zip(message_slots(), outs, strict=True):
        out[...] = message(values, names, slot, off.at[:, slot])


def last_kernel(owner, adjoint, source, local, c0, c1, c2, c3, precond, surf, new, payload):
    values = step(adjoint[...], source[...], local[...], (c0, c1, c2, c3), precond)
    new[...] = values
    count, width = values.shape
    left = sum(placed(values, row, row) for row in range(count))
    contribution = matmul(left, surf[...]).astype(BF16).astype(F32)
    lanes = width // LANES
    tile = [
        contribution[row : row + 1, i * LANES : (i + 1) * LANES]
        for row in range(count)
        for i in range(lanes)
    ]
    tile += [jnp.full((1, LANES), owner[row].astype(F32)) for row in range(count)]
    tile = jnp.concatenate(tile, axis=0)
    for i in range(payload.shape[0]):
        payload[i] = tile


def spread_kernel(got, out):
    peers = got.shape[0]
    lanes = (got.shape[1] - 2) // 2
    lane = lax.broadcasted_iota(jnp.int32, (peers, LANES), 1)
    patch = (lane // CUT["core"]) * (CUT["y"] * CUT["core"] * CUT["x"])
    patch = patch + (lane % CUT["core"]) * CUT["x"]
    patch = patch + lax.axis_index("y") * (CUT["core"] * CUT["x"]) + lax.axis_index("x")
    line = out.shape[0]
    patch = jnp.where(lane < line, patch, -1).astype(F32)
    hot = jnp.concatenate(
        [jnp.where(got[:, 2 * lanes + row, :] == patch, 1.0, 0.0).astype(BF16) for row in range(2)],
        axis=0,
    )
    for i in range(lanes):
        rows = jnp.concatenate([got[:, i, :], got[:, lanes + i, :]], axis=0).astype(BF16)
        sums = lax.dot_general(hot, rows, (((0,), (0,)), ((), ())), preferred_element_type=F32)
        out[:, i, :] = sums[:line]
    for i in range(lanes, out.shape[1]):
        out[:, i, :] = jnp.zeros((line, LANES), F32)


def finish_kernel(grad, parts, out):
    total = jnp.sum(parts[...], axis=0)
    for i in range(grad.shape[1] // LANES):
        where = slice(i * LANES, (i + 1) * LANES)
        out[:, where] = grad[:, where] - total[i : i + 1, :]


def call(kernel, specs, outs, name, flops=0, nbytes=0, scratch=(), vmem=8):
    return pl.pallas_call(
        kernel,
        in_specs=specs,
        out_specs=[VMEM] * len(outs),
        out_shape=outs,
        scratch_shapes=scratch,
        name=name,
        compiler_params=pltpu.CompilerParams(vmem_limit_bytes=vmem << 20),
        cost_estimate=pl.CostEstimate(flops=flops, bytes_accessed=nbytes, transcendentals=0),
    )


def on_device(
    adjoint_start, source, jac_off, jac_diag, precond, surf_map, neighbours, owner, surface_grad
):
    count, width = adjoint_start.shape
    routes = [pairs("dom", 0), pairs("sub", 0), pairs("sub", 1), pairs("dom", 1)]
    block = jax.ShapeDtypeStruct((count, width), F32)

    def swap(messages):
        return [lax.ppermute(m, ALL, route) for m, route in zip(messages, routes, strict=True)]

    matrix = width * width
    messages = call(
        first_kernel,
        [HBM] * 3,
        [block] * 4,
        "first",
        16 * matrix,
        16 * matrix,
        [
            pltpu.SMEM(neighbours.shape, jnp.int32),
            pltpu.VMEM((count, width), F32),
            pltpu.VMEM((4, count, width, width), BF16),
            pltpu.SemaphoreType.DMA((6,)),
        ],
        vmem=63,
    )(neighbours, adjoint_start, jac_off)
    came = swap(messages)
    local_call = call(
        local_kernel, [SMEM, VMEM, VMEM, VMEM], [block], "local", 8 * matrix, 8 * matrix
    )
    (local,) = local_call(neighbours, adjoint_start, jac_off, jac_diag)
    adjoint, *messages = call(
        middle_kernel, [SMEM] + [VMEM] * 9, [block] * 5, "middle", 20 * matrix, 20 * matrix
    )(neighbours, adjoint_start, source, local, *came, precond, jac_off)
    came = swap(messages)
    (local,) = local_call(neighbours, adjoint, jac_off, jac_diag)

    plane = CUT["y"] * CUT["x"]
    line = CUT["z"] * CUT["core"]
    adjoint, payload = call(
        last_kernel,
        [SMEM] + [VMEM] * 9,
        [block, jax.ShapeDtypeStruct((plane, 8, LANES), F32)],
        "last",
        6 * matrix,
        6 * matrix,
    )(owner, adjoint, source, local, *came, precond, surf_map)
    got = lax.all_to_all(payload, ("y", "x"), 0, 0, tiled=True)
    (sums,) = call(
        spread_kernel, [VMEM], [jax.ShapeDtypeStruct((line, 8, LANES), F32)], "spread"
    )(got)
    parts = lax.all_to_all(sums, ("z", "core"), 0, 0, tiled=True)
    (sensitivity,) = call(
        finish_kernel, [VMEM, VMEM], [jax.ShapeDtypeStruct((1, width), F32)], "finish"
    )(surface_grad, parts)
    return (adjoint, sensitivity)


def solution(mesh):
    cut = Mesh(mesh.devices.reshape(tuple(CUT.values())), ALL)
    return jax.shard_map(
        on_device,
        mesh=cut,
        in_specs=(
            P(ALL, None),
            P(ALL, None),
            P(ALL, None, None, None),
            P(ALL, None, None),
            P(ALL, None, None),
            P(),
            P(ALL, None),
            P(ALL),
            P(ALL, None),
        ),
        out_specs=(P(ALL, None), P(ALL, None)),
        check_vma=False,
    )
```

time: 60.1 us -> 54.3 us (0.903)
  blocking collectives: 14.3 us -> 27.3 us
  other arithmetic: 11.3 us -> 0 us
  Pallas kernels: 0 us -> 7.66 us
  waiting for transfers between devices: 8.16 us -> 2.22 us
  starting transfers between devices: 19.3 us -> 14.1 us
  matrix products: 3.17 us -> 0 us
    all_to_all x0 -> x1, blocking collectives: none -> 9.98 us  [on_device(): got = lax.all_to_all(payload, ('y', 'x'), 0, 0, tiled=True)]
    pallas_call x0 -> x7, Pallas kernels: none -> 7.66 us  [the longest x1 2.67 us: on_device(): call(first_kernel, [HBM] * 3, [block] * 4, 'first', 16 * matrix, 16 * mat...]
    all_to_all x1 -> x0, waiting for transfers between devices: 6.37 us -> none  [on_device(): lax.all_to_all(jnp.broadcast_to(tagged[None], (plane, row_count, width +...]
    reduce_sum x11 -> x0, other arithmetic: 3.55 us -> none  [the longest x10 3.51 us: collect(): return jnp.sum(spread, axis=0)]
    all_to_all x1 -> x0, starting transfers between devices: 3.5 us -> none  [on_device(): lax.all_to_all(jnp.broadcast_to(tagged[None], (plane, row_count, width +...]
    dot_general x8 -> x0, matrix products: 3.17 us -> none  [the longest x2 1.45 us: on_device(): jnp.einsum('rb,rbc->rc', residual_low, precond, preferred_element_type=jn...]
    all_to_all x1, blocking collectives: 14.3 us -> 17.3 us  [on_device(): parts = lax.all_to_all(sums, ('z', 'core'), 0, 0, tiled=True)]
    convert_element_type x6 -> x0, other arithmetic: 2.27 us -> none  [the longest x1 0.74 us: on_device(): owner.astype(jnp.bfloat16)[:, None]]
  transfers between devices with their start and end apart: 9 -> 8, of which waited for: 3 -> 2; matrix products, arithmetic and copies ran while one was open for 8% -> 0% of each run, Pallas kernels for 0% -> 3%
where the time goes in v2:
time: 54.3 us; the launch traced here: 54.1 us
  blocking collectives  27.3 us (50%)
  starting transfers between devices  14.1 us (26%)
  Pallas kernels  7.66 us (14%)
  waiting for transfers between devices  2.22 us (4%)
  local copies, waits for them, and re-layouts  2.02 us (4%)
  between operations  0.75 us (1%)
    all_to_all x1, blocking collectives, on_device(): parts = lax.all_to_all(sums, ('z', 'core'), 0, 0, tiled=True)  17.3 us
    ppermute x8, starting transfers between devices, swap(): lax.ppermute(m, ALL, route)  14.1 us
    all_to_all x1, blocking collectives, on_device(): got = lax.all_to_all(payload, ('y', 'x'), 0, 0, tiled=True)  9.98 us
    pallas_call x1, Pallas kernels, on_device(): call(first_kernel, [HBM] * 3, [block] * 4, 'first', 16 * matrix, 16 * mat...  2.67 us
    ppermute x8, waiting for transfers between devices, swap(): lax.ppermute(m, ALL, route)  2.22 us
    unnamed x20, local copies, waits for them, and re-layouts  2.02 us
    pallas_call x1, Pallas kernels, on_device(): call(last_kernel, [SMEM] + [VMEM] * 9, [block, jax.ShapeDtypeStruct((plan...  1.33 us
    pallas_call x1, Pallas kernels, on_device(): call(middle_kernel, [SMEM] + [VMEM] * 9, [block] * 5, 'middle', 20 * matr...  1.18 us
  transfers between devices with their start and end apart: 8, of which 2 were waited for; matrix products, arithmetic and copies ran while one was open for 0% of the time, Pallas kernels for 3%

profile of v2, /device:TPU:1, one launch (start us, length us, event | category | flops | bytes accessed | tf_op | source)
XLA Modules:
  0.0 54.1 jit_solution(10130774095245654419)
XLA Ops:
  0.7 2.7 %first.1 = (f32[2,384]{1,0:T(2,128)}, f32[2,384]{1,0:T(2,128)}, f32[2,384]{1,0:T(2,128)}, f32[2,384]{1,0:T(2,128)}) custom-call(s32[2,5]{1,0:T(2,128)} %names.5, f32[2,384]{1,0:T(2,128)} %adjoint.3, bf16[2,5,384,384]{3,2,1,0:T(8,128)(2,1)} %off.5), custom_call_target="tpu_custom_call" | custom-call | flops 2359296 | bytes 2359296 | tf_op jit(solution)/shard_map/first/pallas_call | solution.py:172
  3.3 3.3 %collective-permute-start = (f32[2,384]{1,0:T(2,128)}, f32[2,384]{1,0:T(2,128)S(1)}, u32[]{:S(2)}, u32[]{:S(2)}) collective-permute-start(f32[2,384]{1,0:T(2,128)} %get-tuple-element.13), channel_id=1, source_target_pairs={{0,4},{1,5},{2,6},{3,7},{4,0},{5,1},{6,2},{7,3},{8,12},{9,13},{10,... | collective-permute-start | bytes 9224 | tf_op jit(solution)/shard_map/ppermute | solution.py:169
  6.7 0.0 collective-permute-start.1
  6.7 1.3 %collective-permute-start.2 = (f32[2,384]{1,0:T(2,128)}, f32[2,384]{1,0:T(2,128)S(1)}, u32[]{:S(2)}, u32[]{:S(2)}) collective-permute-start(f32[2,384]{1,0:T(2,128)} %get-tuple-element.15), channel_id=1, source_target_pairs={{0,3},{1,2},{2,1},{3,0},{4,7},{5,6},{6,5},{7,4},{8,11},{9,10},{10,... | collective-permute-start | bytes 9224 | tf_op jit(solution)/shard_map/ppermute | solution.py:169
  8.0 1.8 %collective-permute-start.3 = (f32[2,384]{1,0:T(2,128)}, f32[2,384]{1,0:T(2,128)S(1)}, u32[]{:S(2)}, u32[]{:S(2)}) collective-permute-start(f32[2,384]{1,0:T(2,128)} %get-tuple-element.16), channel_id=1, source_target_pairs={{0,252},{1,253},{2,254},{3,255},{4,8},{5,9},{6,10},{7,11},{8,4},{9... | collective-permute-start | bytes 9224 | tf_op jit(solution)/shard_map/ppermute | solution.py:169
  9.8 1.8 %copy-done = bf16[2,5,384,384]{3,2,1,0:T(8,128)(2,1)S(1)} copy-done((bf16[2,5,384,384]{3,2,1,0:T(8,128)(2,1)S(1)}, bf16[2,5,384,384]{3,2,1,0:T(8,128)(2,1)}, u32[]{:S(2)}) %copy-start) | copy-done | bytes 2949144
  11.7 0.8 %local.2 = f32[2,384]{1,0:T(2,128)S(1)} custom-call(s32[2,5]{1,0:T(2,128)S(1)} %copy-done.6, f32[2,384]{1,0:T(2,128)S(1)} %copy-done.5, bf16[2,5,384,384]{3,2,1,0:T(8,128)(2,1)S(1)} %copy-done, bf16[2,384,384]{2,1,0:T(8,128)(2,1)S(1)} %copy-done.2), custom_call_target="tpu_custom_call" | custom-call | flops 1179648 | bytes 1179648 | tf_op jit(solution)/shard_map/local/pallas_call | solution.py:191
  12.5 0.0 collective-permute-done.c0
  12.5 0.0 collective-permute-done.1.c1
  12.5 0.0 collective-permute-done.3.c3
  12.6 0.2 copy-done.3
  12.7 1.2 %middle.1 = (f32[2,384]{1,0:T(2,128)S(1)}, f32[2,384]{1,0:T(2,128)S(1)}, f32[2,384]{1,0:T(2,128)S(1)}, f32[2,384]{1,0:T(2,128)S(1)}, f32[2,384]{1,0:T(2,128)S(1)}) custom-call(s32[2,5]{1,0:T(2,128)S(1)} %copy-done.6, f32[2,384]{1,0:T(2,128)S(1)} %copy-done.5, f32[2,384]{1,0:T(2,128)S(1)} %copy-done.7, f32[2,384]{1,0:T(2,128)S(1)} %local.2, ...), custom_call_target="tpu_custom_call" | custom-call | flops 2949120 | bytes 2949120 | tf_op jit(solution)/shard_map/middle/pallas_call | solution.py:192
  13.9 6.7 %collective-permute-start.4 = (f32[2,384]{1,0:T(2,128)S(1)}, f32[2,384]{1,0:T(2,128)S(1)}, u32[]{:S(2)}, u32[]{:S(2)}) collective-permute-start(f32[2,384]{1,0:T(2,128)S(1)} %get-tuple-element.18), channel_id=1, source_target_pairs={{0,4},{1,5},{2,6},{3,7},{4,0},{5,1},{6,2},{7,3},{8,12},{9,13},{10,... | collective-permute-start | bytes 9224 | tf_op jit(solution)/shard_map/ppermute | solution.py:169
  20.6 0.3 collective-permute-start.5
  20.9 0.6 %collective-permute-start.6 = (f32[2,384]{1,0:T(2,128)S(1)}, f32[2,384]{1,0:T(2,128)S(1)}, u32[]{:S(2)}, u32[]{:S(2)}) collective-permute-start(f32[2,384]{1,0:T(2,128)S(1)} %get-tuple-element.20), channel_id=1, source_target_pairs={{0,3},{1,2},{2,1},{3,0},{4,7},{5,6},{6,5},{7,4},{8,11},{9,10},{10,... | collective-permute-start | bytes 9224 | tf_op jit(solution)/shard_map/ppermute | solution.py:169
  21.5 0.0 collective-permute-start.7
  21.5 0.8 %local.3 = f32[2,384]{1,0:T(2,128)S(1)} custom-call(s32[2,5]{1,0:T(2,128)S(1)} %copy-done.6, f32[2,384]{1,0:T(2,128)S(1)} %get-tuple-element.17.adjoint, bf16[2,5,384,384]{3,2,1,0:T(8,128)(2,1)S(1)} %copy-done.1, bf16[2,384,384]{2,1,0:T(8,128)(2,1)S(1)} %copy-done.2), custom_call_target="tpu_custom_call" | custom-call | flops 1179648 | bytes 1179648 | tf_op jit(solution)/shard_map/local/pallas_call | solution.py:196
  22.4 0.7 %collective-permute-done.5.c1 = f32[2,384]{1,0:T(2,128)S(1)} collective-permute-done((f32[2,384]{1,0:T(2,128)S(1)}, f32[2,384]{1,0:T(2,128)S(1)}, u32[]{:S(2)}, u32[]{:S(2)}) %collective-permute-start.5) | collective-permute-done | bytes 3104 | tf_op jit(solution)/shard_map/ppermute | solution.py:169
  23.0 1.5 %collective-permute-done.6.c2 = f32[2,384]{1,0:T(2,128)S(1)} collective-permute-done((f32[2,384]{1,0:T(2,128)S(1)}, f32[2,384]{1,0:T(2,128)S(1)}, u32[]{:S(2)}, u32[]{:S(2)}) %collective-permute-start.6) | collective-permute-done | bytes 3104 | tf_op jit(solution)/shard_map/ppermute | solution.py:169
  24.6 1.3 %last.1 = (f32[2,384]{1,0:T(2,128)}, f32[16,8,128]{2,1,0:T(8,128)S(1)}) custom-call(s32[2]{0:T(128)S(1)} %copy-done.9, f32[2,384]{1,0:T(2,128)S(1)} %get-tuple-element.17.adjoint, f32[2,384]{1,0:T(2,128)S(1)} %copy-done.7, f32[2,384]{1,0:T(2,128)S(1)} %local.3, f32[2,384]{1,0:T(2,128)S(1)} %collective-permute-done.4.c0, ...), custom_call_target="tpu_custom_call" | custom-call | flops 884736 | bytes 884736 | tf_op jit(solution)/shard_map/last/pallas_call | solution.py:200
  25.9 10.0 %all_to_all.10.got = f32[16,8,128]{2,1,0:T(8,128)S(1)} all-to-all(f32[16,8,128]{2,1,0:T(8,128)S(1)} %get-tuple-element.23), channel_id=1, replica_groups=mesh['z'=8,'y'=4,'core'=2,'x'=4] {'y','x'}, dimensions={0} | all-to-all | bytes 131072 | tf_op jit(solution)/shard_map/all_to_all | solution.py:208
  35.9 0.2 spread.1
  36.1 17.3 %all_to_all.11.parts = f32[16,8,128]{2,1,0:T(8,128)S(1)} all-to-all(f32[16,8,128]{2,1,0:T(8,128)S(1)} %spread.1), channel_id=1, replica_groups=mesh['z'=8,'y'=4,'core'=2,'x'=4] {'z','core'}, dimensions={0} | all-to-all | bytes 131072 | tf_op jit(solution)/shard_map/all_to_all | solution.py:212
  53.5 0.6 %finish.1 = f32[1,384]{1,0:T(1,128)} custom-call(f32[1,384]{1,0:T(1,128)S(1)} %copy-done.8, f32[16,8,128]{2,1,0:T(8,128)S(1)} %all_to_all.11.parts), custom_call_target="tpu_custom_call" | custom-call | tf_op jit(solution)/shard_map/finish/pallas_call | solution.py:213
  (21 shorter events, 0.0 us)
Async XLA Ops:
  0.6 9.2 %copy-start.6 = (s32[2,5]{1,0:T(2,128)S(1)}, s32[2,5]{1,0:T(2,128)}, u32[]{:S(2)}) copy-start(s32[2,5]{1,0:T(2,128)} %names.5) | copy-start | bytes 124
  0.6 9.2 %copy-start.5 = (f32[2,384]{1,0:T(2,128)S(1)}, f32[2,384]{1,0:T(2,128)}, u32[]{:S(2)}) copy-start(f32[2,384]{1,0:T(2,128)} %adjoint.3) | copy-start | bytes 9220
  0.7 9.2 %copy-start.2 = (bf16[2,384,384]{2,1,0:T(8,128)(2,1)S(1)}, bf16[2,384,384]{2,1,0:T(8,128)(2,1)}, u32[]{:S(2)}) copy-start(bf16[2,384,384]{2,1,0:T(8,128)(2,1)} %diag.3) | copy-start | bytes 1769476
  0.7 11.9 %copy-start.7 = (f32[2,384]{1,0:T(2,128)S(1)}, f32[2,384]{1,0:T(2,128)}, u32[]{:S(2)}) copy-start(f32[2,384]{1,0:T(2,128)} %source.3) | copy-start | bytes 9220
  3.3 9.2 %collective-permute-start = (f32[2,384]{1,0:T(2,128)}, f32[2,384]{1,0:T(2,128)S(1)}, u32[]{:S(2)}, u32[]{:S(2)}) collective-permute-start(f32[2,384]{1,0:T(2,128)} %get-tuple-element.13), channel_id=1, source_target_pairs={{0,4},{1,5},{2,6},{3,7},{4,0},{5,1},{6,2},{7,3},{8,12},{9,13},{10,... | collective-permute-start | bytes 9224 | tf_op jit(solution)/shard_map/ppermute | solution.py:169
  6.7 5.8 %collective-permute-start.1 = (f32[2,384]{1,0:T(2,128)}, f32[2,384]{1,0:T(2,128)S(1)}, u32[]{:S(2)}, u32[]{:S(2)}) collective-permute-start(f32[2,384]{1,0:T(2,128)} %get-tuple-element.14), channel_id=1, source_target_pairs={{0,1},{1,0},{2,3},{3,2},{4,5},{5,4},{6,7},{7,6},{8,9},{9,8},{10,11... | collective-permute-start | bytes 9224 | tf_op jit(solution)/shard_map/ppermute | solution.py:169
  6.7 5.8 %collective-permute-start.2 = (f32[2,384]{1,0:T(2,128)}, f32[2,384]{1,0:T(2,128)S(1)}, u32[]{:S(2)}, u32[]{:S(2)}) collective-permute-start(f32[2,384]{1,0:T(2,128)} %get-tuple-element.15), channel_id=1, source_target_pairs={{0,3},{1,2},{2,1},{3,0},{4,7},{5,6},{6,5},{7,4},{8,11},{9,10},{10,... | collective-permute-start | bytes 9224 | tf_op jit(solution)/shard_map/ppermute | solution.py:169
  8.0 4.5 %collective-permute-start.3 = (f32[2,384]{1,0:T(2,128)}, f32[2,384]{1,0:T(2,128)S(1)}, u32[]{:S(2)}, u32[]{:S(2)}) collective-permute-start(f32[2,384]{1,0:T(2,128)} %get-tuple-element.16), channel_id=1, source_target_pairs={{0,252},{1,253},{2,254},{3,255},{4,8},{5,9},{6,10},{7,11},{8,4},{9... | collective-permute-start | bytes 9224 | tf_op jit(solution)/shard_map/ppermute | solution.py:169
  9.8 1.8 %copy-start = (bf16[2,5,384,384]{3,2,1,0:T(8,128)(2,1)S(1)}, bf16[2,5,384,384]{3,2,1,0:T(8,128)(2,1)}, u32[]{:S(2)}) copy-start(bf16[2,5,384,384]{3,2,1,0:T(8,128)(2,1)} %off.5) | copy-start | bytes 8847364
  11.7 1.1 %copy-start.3 = (bf16[2,384,384]{2,1,0:T(8,128)(2,1)S(1)}, bf16[2,384,384]{2,1,0:T(8,128)(2,1)}, u32[]{:S(2)}) copy-start(bf16[2,384,384]{2,1,0:T(8,128)(2,1)} %precond.3) | copy-start | bytes 1769476
  11.7 9.9 %copy-start.1 = (bf16[2,5,384,384]{3,2,1,0:T(8,128)(2,1)S(1)}, bf16[2,5,384,384]{3,2,1,0:T(8,128)(2,1)}, u32[]{:S(2)}) copy-start(bf16[2,5,384,384]{3,2,1,0:T(8,128)(2,1)} %off.5) | copy-start | bytes 8847364
  12.5 12.1 %copy-start.4 = (bf16[384,384]{1,0:T(8,128)(2,1)S(1)}, bf16[384,384]{1,0:T(8,128)(2,1)}, u32[]{:S(2)}) copy-start(bf16[384,384]{1,0:T(8,128)(2,1)} %surf.1) | copy-start | bytes 884740
  12.5 12.1 %copy-start.9 = (s32[2]{0:T(128)S(1)}, s32[2]{0:T(128)}, u32[]{:S(2)}) copy-start(s32[2]{0:T(128)} %owner.1) | copy-start | bytes 28
  13.9 39.6 %copy-start.8 = (f32[1,384]{1,0:T(1,128)S(1)}, f32[1,384]{1,0:T(1,128)}, u32[]{:S(2)}) copy-start(f32[1,384]{1,0:T(1,128)} %grad.1) | copy-start | bytes 4612
  13.9 8.5 %collective-permute-start.4 = (f32[2,384]{1,0:T(2,128)S(1)}, f32[2,384]{1,0:T(2,128)S(1)}, u32[]{:S(2)}, u32[]{:S(2)}) collective-permute-start(f32[2,384]{1,0:T(2,128)S(1)} %get-tuple-element.18), channel_id=1, source_target_pairs={{0,4},{1,5},{2,6},{3,7},{4,0},{5,1},{6,2},{7,3},{8,12},{9,13},{10,... | collective-permute-start | bytes 9224 | tf_op jit(solution)/shard_map/ppermute | solution.py:169
  20.6 2.5 %collective-permute-start.5 = (f32[2,384]{1,0:T(2,128)S(1)}, f32[2,384]{1,0:T(2,128)S(1)}, u32[]{:S(2)}, u32[]{:S(2)}) collective-permute-start(f32[2,384]{1,0:T(2,128)S(1)} %get-tuple-element.19), channel_id=1, source_target_pairs={{0,1},{1,0},{2,3},{3,2},{4,5},{5,4},{6,7},{7,6},{8,9},{9,8},{10,11... | collective-permute-start | bytes 9224 | tf_op jit(solution)/shard_map/ppermute | solution.py:169
  20.9 3.7 %collective-permute-start.6 = (f32[2,384]{1,0:T(2,128)S(1)}, f32[2,384]{1,0:T(2,128)S(1)}, u32[]{:S(2)}, u32[]{:S(2)}) collective-permute-start(f32[2,384]{1,0:T(2,128)S(1)} %get-tuple-element.20), channel_id=1, source_target_pairs={{0,3},{1,2},{2,1},{3,0},{4,7},{5,6},{6,5},{7,4},{8,11},{9,10},{10,... | collective-permute-start | bytes 9224 | tf_op jit(solution)/shard_map/ppermute | solution.py:169
  21.5 3.1 %collective-permute-start.7 = (f32[2,384]{1,0:T(2,128)S(1)}, f32[2,384]{1,0:T(2,128)S(1)}, u32[]{:S(2)}, u32[]{:S(2)}) collective-permute-start(f32[2,384]{1,0:T(2,128)S(1)} %get-tuple-element.21), channel_id=1, source_target_pairs={{0,252},{1,253},{2,254},{3,255},{4,8},{5,9},{6,10},{7,11},{8,4},{9... | collective-permute-start | bytes 9224 | tf_op jit(solution)/shard_map/ppermute | solution.py:169

commit v3 on v2

v3 whole, which is shorter than its diff:
```python
import math

import jax
import jax.numpy as jnp
from jax import lax
from jax.experimental import pallas as pl
from jax.experimental.pallas import tpu as pltpu
from jax.sharding import Mesh, PartitionSpec as P

CUT = {"z": 8, "y": 4, "core": 2, "x": 4}
ALL = tuple(CUT)
LANES = 128
FIRST, SECOND = ('z', 'core'), ('y', 'x')
ORDER = (3, 1, 2, 0)
F32 = jnp.float32
BF16 = jnp.bfloat16
VMEM = pl.BlockSpec(memory_space=pltpu.VMEM)
HBM = pl.BlockSpec(memory_space=pltpu.HBM)


def pairs(axis, first):
    subs = CUT["x"]
    devices = CUT["z"] * CUT["y"] * CUT["core"] * subs
    route = []
    for device in range(devices):
        dom, sub = divmod(device, subs)
        if axis == "dom":
            doms = devices // subs
            dom = (((dom - first) % doms ^ 1) + first) % doms
        else:
            sub = (((sub - first) % subs ^ 1) + first) % subs
        route.append((device, dom * subs + sub))
    return route


def placed(row, count, target):
    rows = lax.broadcasted_iota(jnp.int32, (count, row.shape[1]), 0)
    return jnp.where(rows == target, row, 0.0).astype(BF16)


def matmul(left, right):
    return jnp.dot(left, right, preferred_element_type=F32)


def message_slots():
    core, odd = lax.axis_index("core"), lax.axis_index("x") % 2
    four = (1, 2, core), (3, 4, odd), (4, 3, odd), (2, 1, core)
    return [four[i] for i in ORDER]


def step(adjoint, source, local, came, precond_ref):
    residual = source - local
    for part in came:
        residual = residual - part[...]
    count = adjoint.shape[0]
    for row in range(count):
        left = placed(residual[row : row + 1, :], count, row)
        adjoint = adjoint + matmul(left, precond_ref[row])
    return adjoint


def send_all(values, names, off, outs):
    count = values.shape[0]
    for (even, odd, which), out, blocks in zip(message_slots(), outs, off, strict=True):
        total = jnp.zeros(out.shape, F32)
        for row in range(count):
            here = slice(row, row + 1)
            name = jnp.where(which == 0, names[here, even : even + 1], names[here, odd : odd + 1])
            left = placed(values[here, :], count, name % count)
            total = total + matmul(left, blocks(row))
        out[...] = total


def first_kernel(names_in, adjoint_in, off_in, c0, c1, c2, c3, off, names, adjoint, sems):
    slots = [jnp.where(which == 0, even, odd) for even, odd, which in message_slots()]
    heads = [
        pltpu.make_async_copy(names_in, names, sems.at[5]),
        pltpu.make_async_copy(adjoint_in, adjoint, sems.at[6]),
    ]
    blocks = [
        pltpu.make_async_copy(off_in.at[:, slot], off.at[:, slot], sems.at[m])
        for m, slot in enumerate(slots + [0])
    ]
    for copy in heads + blocks:
        copy.start()
    for copy in heads:
        copy.wait()

    def arrived(m, slot):
        def block(row):
            if row == 0:
                blocks[m].wait()
            return off[row, slot]

        return block

    send_all(
        adjoint[...], names, [arrived(m, slot) for m, slot in enumerate(slots)], (c0, c1, c2, c3)
    )
    blocks[-1].wait()


def local_kernel(names, adjoint, off, diag, out):
    count = adjoint.shape[0]
    total = jnp.zeros(out.shape, F32)
    for row in range(count):
        values = adjoint[row : row + 1, :]
        total = total + matmul(placed(values, count, names[row : row + 1, 0:1] % count), off[row, 0])
        total = total + matmul(placed(values, count, row), diag[row])
    out[...] = total


def middle_kernel(names, adjoint, source, local, c0, c1, c2, c3, precond, off, new, *outs):
    values = step(adjoint[...], source[...], local[...], (c0, c1, c2, c3), precond)
    new[...] = values
    slots = [jnp.where(which == 0, even, odd) for even, odd, which in message_slots()]
    send_all(values, names, [lambda row, slot=slot: off[row, slot] for slot in slots], outs)


def last_kernel(owner, adjoint, source, local, c0, c1, c2, c3, precond, surf, new, payload):
    values = step(adjoint[...], source[...], local[...], (c0, c1, c2, c3), precond)
    new[...] = values
    count, width = values.shape
    contribution = matmul(values.astype(BF16), surf[...]).astype(BF16).astype(F32)
    tile = [
        contribution[row : row + 1, i * LANES : (i + 1) * LANES]
        for row in range(count)
        for i in range(width // LANES)
    ]
    tile += [
        jnp.broadcast_to(owner[0:1, row : row + 1].astype(F32), (1, LANES)) for row in range(count)
    ]
    tile = jnp.concatenate(tile, axis=0)
    for i in range(payload.shape[0]):
        payload[i] = tile


def stride(axis):
    step = 1
    for name in reversed(ALL):
        if name == axis:
            return step
        step *= CUT[name]
    raise ValueError(axis)


def spread_kernel(got, out):
    peers = got.shape[0]
    lanes = (got.shape[1] - 2) // 2
    lane = lax.broadcasted_iota(jnp.int32, (peers, LANES), 1)
    patch = sum(lax.axis_index(axis) * stride(axis) for axis in FIRST)
    place = lane
    for axis in reversed(SECOND):
        patch = patch + place % CUT[axis] * stride(axis)
        place = place // CUT[axis]
    group = out.shape[0]
    patch = jnp.where(lane < group, patch, -1).astype(F32)
    hot = jnp.concatenate(
        [jnp.where(got[:, 2 * lanes + row, :] == patch, 1.0, 0.0).astype(BF16) for row in range(2)],
        axis=0,
    )
    for i in range(lanes):
        rows = jnp.concatenate([got[:, i, :], got[:, lanes + i, :]], axis=0).astype(BF16)
        sums = lax.dot_general(hot, rows, (((0,), (0,)), ((), ())), preferred_element_type=F32)
        out[:, i, :] = sums[:group]
    for i in range(lanes, out.shape[1]):
        out[:, i, :] = jnp.zeros((group, LANES), F32)


def finish_kernel(grad, parts, out):
    total = jnp.sum(parts[...], axis=0)
    for i in range(grad.shape[1] // LANES):
        where = slice(i * LANES, (i + 1) * LANES)
        out[:, where] = grad[:, where] - total[i : i + 1, :]


def call(kernel, specs, outs, name, flops=0, nbytes=0, scratch=(), vmem=8):
    return pl.pallas_call(
        kernel,
        in_specs=specs,
        out_specs=[VMEM] * len(outs),
        out_shape=outs,
        scratch_shapes=scratch,
        name=name,
        compiler_params=pltpu.CompilerParams(vmem_limit_bytes=vmem << 20),
        cost_estimate=pl.CostEstimate(flops=flops, bytes_accessed=nbytes, transcendentals=0),
    )


def on_device(
    adjoint_start, source, jac_off, jac_diag, precond, surf_map, neighbours, owner, surface_grad
):
    count, width = adjoint_start.shape
    routes = [pairs("dom", 0), pairs("sub", 0), pairs("sub", 1), pairs("dom", 1)]
    routes = [routes[i] for i in ORDER]
    block = jax.ShapeDtypeStruct((count, width), F32)

    def swap(messages):
        return [lax.ppermute(m, ALL, route) for m, route in zip(messages, routes, strict=True)]

    matrix = width * width
    *messages, off = call(
        first_kernel,
        [HBM] * 3,
        [pltpu.VMEM((count, width), F32)] * 4 + [pltpu.VMEM(jac_off.shape, BF16)],
        "first",
        16 * matrix,
        16 * matrix,
        [
            pltpu.VMEM(neighbours.shape, jnp.int32),
            pltpu.VMEM((count, width), F32),
            pltpu.SemaphoreType.DMA((7,)),
        ],
        52,
    )(neighbours, adjoint_start, jac_off)
    came = swap(messages)
    local_call = call(local_kernel, [VMEM] * 4, [block], "local", 8 * matrix, 8 * matrix)
    (local,) = local_call(neighbours, adjoint_start, off, jac_diag)
    adjoint, *messages = call(
        middle_kernel, [VMEM] * 10, [block] * 5, "middle", 20 * matrix, 20 * matrix
    )(neighbours, adjoint_start, source, local, *came, precond, off)
    came = swap(messages)
    (local,) = local_call(neighbours, adjoint, off, jac_diag)

    plane = math.prod(CUT[axis] for axis in FIRST)
    line = math.prod(CUT[axis] for axis in SECOND)
    adjoint, payload = call(
        last_kernel,
        [VMEM] * 10,
        [block, jax.ShapeDtypeStruct((plane, 8, LANES), F32)],
        "last",
        6 * matrix,
        6 * matrix,
    )(owner.reshape(1, count), adjoint, source, local, *came, precond, surf_map)
    got = lax.all_to_all(payload, FIRST, 0, 0, tiled=True)
    (sums,) = call(
        spread_kernel, [VMEM], [jax.ShapeDtypeStruct((line, 8, LANES), F32)], "spread"
    )(got)
    parts = lax.all_to_all(sums, SECOND, 0, 0, tiled=True)
    (sensitivity,) = call(
        finish_kernel, [VMEM, VMEM], [jax.ShapeDtypeStruct((1, width), F32)], "finish"
    )(surface_grad, parts)
    return (adjoint, sensitivity)


def solution(mesh):
    cut = Mesh(mesh.devices.reshape(tuple(CUT.values())), ALL)
    return jax.shard_map(
        on_device,
        mesh=cut,
        in_specs=(
            P(ALL, None),
            P(ALL, None),
            P(ALL, None, None, None),
            P(ALL, None, None),
            P(ALL, None, None),
            P(),
            P(ALL, None),
            P(ALL),
            P(ALL, None),
        ),
        out_specs=(P(ALL, None), P(ALL, None)),
        check_vma=False,
    )
```

time: 54.3 us -> 48.8 us (0.90)
  blocking collectives: 27.3 us -> 22.8 us
  starting transfers between devices: 14.1 us -> 18.5 us
  Pallas kernels: 7.66 us -> 5.56 us
  local copies, waits for them, and re-layouts: 2.02 us -> 0.03 us
  waiting for transfers between devices: 2.22 us -> 1.02 us
    all_to_all x2, blocking collectives: 27.3 us -> 22.8 us  [the longest x1 12.3 us: on_device(): got = lax.all_to_all(payload, FIRST, 0, 0, tiled=True)]
    ppermute x8, starting transfers between devices: 14.1 us -> 18.5 us  [swap(): lax.ppermute(m, ALL, route)]
    pallas_call x5, Pallas kernels: 6.84 us -> 4.74 us  [the longest x1 2.73 us: on_device(): call(first_kernel, [HBM] * 3, [pltpu.VMEM((count, width), F32)] * 4 + [pl...]
    unnamed x20 -> x16, local copies, waits for them, and re-layouts: 2.02 us -> 0.03 us
    ppermute x8, waiting for transfers between devices: 2.22 us -> 1.02 us  [swap(): lax.ppermute(m, ALL, route)]
  transfers between devices with their start and end apart: 8 -> 8, of which waited for: 2 -> 2; matrix products, arithmetic and copies ran while one was open for 0% -> 0% of each run, Pallas kernels for 3% -> 1%
where the time goes in v3:
time: 48.8 us; the launch traced here: 48.7 us
  blocking collectives  22.8 us (47%)
  starting transfers between devices  18.5 us (38%)
  Pallas kernels  5.56 us (11%)
  waiting for transfers between devices  1.02 us (2%)
  between operations  0.75 us (2%)
    ppermute x8, starting transfers between devices, swap(): lax.ppermute(m, ALL, route)  18.5 us
    all_to_all x1, blocking collectives, on_device(): got = lax.all_to_all(payload, FIRST, 0, 0, tiled=True)  12.3 us
    all_to_all x1, blocking collectives, on_device(): parts = lax.all_to_all(sums, SECOND, 0, 0, tiled=True)  10.5 us
    pallas_call x1, Pallas kernels, on_device(): call(first_kernel, [HBM] * 3, [pltpu.VMEM((count, width), F32)] * 4 + [pl...  2.73 us
    ppermute x8, waiting for transfers between devices, swap(): lax.ppermute(m, ALL, route)  1.02 us
  transfers between devices with their start and end apart: 8, of which 2 were waited for; matrix products, arithmetic and copies ran while one was open for 0% of the time, Pallas kernels for 1%

profile of v3, /device:TPU:1, one launch (start us, length us, event | category | flops | bytes accessed | tf_op | source)
XLA Modules:
  0.0 48.7 jit_solution(10360786488210303774)
XLA Ops:
  0.7 2.7 %first.1 = (f32[2,384]{1,0:T(2,128)S(1)}, f32[2,384]{1,0:T(2,128)S(1)}, f32[2,384]{1,0:T(2,128)S(1)}, f32[2,384]{1,0:T(2,128)S(1)}, bf16[2,5,384,384]{3,2,1,0:T(8,128)(2,1)S(1)}) custom-call(s32[2,5]{1,0:T(2,128)} %names.5, f32[2,384]{1,0:T(2,128)} %adjoint.3, bf16[2,5,384,384]{3,2,1,0:T(8,128)(2,1)} %off_in.1), custom_call_target="tpu_custom_call" | custom-call | flops 2359296 | bytes 2359296 | tf_op jit(solution)/shard_map/first/pallas_call | solution.py:202
  3.4 2.8 %collective-permute-start = (f32[2,384]{1,0:T(2,128)S(1)}, f32[2,384]{1,0:T(2,128)S(1)}, u32[]{:S(2)}, u32[]{:S(2)}) collective-permute-start(f32[2,384]{1,0:T(2,128)S(1)} %get-tuple-element.15), channel_id=1, source_target_pairs={{0,252},{1,253},{2,254},{3,255},{4,8},{5,9},{6,10},{7,11},{8,4},{9... | collective-permute-start | bytes 9224 | tf_op jit(solution)/shard_map/ppermute | solution.py:199
  6.2 1.2 %collective-permute-start.1 = (f32[2,384]{1,0:T(2,128)S(1)}, f32[2,384]{1,0:T(2,128)S(1)}, u32[]{:S(2)}, u32[]{:S(2)}) collective-permute-start(f32[2,384]{1,0:T(2,128)S(1)} %get-tuple-element.16), channel_id=1, source_target_pairs={{0,1},{1,0},{2,3},{3,2},{4,5},{5,4},{6,7},{7,6},{8,9},{9,8},{10,11... | collective-permute-start | bytes 9224 | tf_op jit(solution)/shard_map/ppermute | solution.py:199
  7.4 1.8 %collective-permute-start.2 = (f32[2,384]{1,0:T(2,128)S(1)}, f32[2,384]{1,0:T(2,128)S(1)}, u32[]{:S(2)}, u32[]{:S(2)}) collective-permute-start(f32[2,384]{1,0:T(2,128)S(1)} %get-tuple-element.17), channel_id=1, source_target_pairs={{0,3},{1,2},{2,1},{3,0},{4,7},{5,6},{6,5},{7,4},{8,11},{9,10},{10,... | collective-permute-start | bytes 9224 | tf_op jit(solution)/shard_map/ppermute | solution.py:199
  9.2 7.1 %collective-permute-start.3 = (f32[2,384]{1,0:T(2,128)S(1)}, f32[2,384]{1,0:T(2,128)S(1)}, u32[]{:S(2)}, u32[]{:S(2)}) collective-permute-start(f32[2,384]{1,0:T(2,128)S(1)} %get-tuple-element.18), channel_id=1, source_target_pairs={{0,4},{1,5},{2,6},{3,7},{4,0},{5,1},{6,2},{7,3},{8,12},{9,13},{10,... | collective-permute-start | bytes 9224 | tf_op jit(solution)/shard_map/ppermute | solution.py:199
  16.4 0.3 local.2
  16.6 0.0 collective-permute-done.c0
  16.7 0.0 collective-permute-done.1.c1
  16.7 0.5 collective-permute-done.3.c3
  17.2 0.7 %middle.1 = (f32[2,384]{1,0:T(2,128)S(1)}, f32[2,384]{1,0:T(2,128)S(1)}, f32[2,384]{1,0:T(2,128)S(1)}, f32[2,384]{1,0:T(2,128)S(1)}, f32[2,384]{1,0:T(2,128)S(1)}) custom-call(s32[2,5]{1,0:T(2,128)S(1)} %copy-done.4, f32[2,384]{1,0:T(2,128)S(1)} %copy-done.3, f32[2,384]{1,0:T(2,128)S(1)} %copy-done.5, f32[2,384]{1,0:T(2,128)S(1)} %local.2, ...), custom_call_target="tpu_custom_call" | custom-call | flops 2949120 | bytes 2949120 | tf_op jit(solution)/shard_map/middle/pallas_call | solution.py:219
  17.8 0.1 collective-permute-start.4
  17.9 0.4 collective-permute-start.5
  18.3 0.6 %collective-permute-start.6 = (f32[2,384]{1,0:T(2,128)S(1)}, f32[2,384]{1,0:T(2,128)S(1)}, u32[]{:S(2)}, u32[]{:S(2)}) collective-permute-start(f32[2,384]{1,0:T(2,128)S(1)} %get-tuple-element.22), channel_id=1, source_target_pairs={{0,3},{1,2},{2,1},{3,0},{4,7},{5,6},{6,5},{7,4},{8,11},{9,10},{10,... | collective-permute-start | bytes 9224 | tf_op jit(solution)/shard_map/ppermute | solution.py:199
  19.0 4.5 %collective-permute-start.7 = (f32[2,384]{1,0:T(2,128)S(1)}, f32[2,384]{1,0:T(2,128)S(1)}, u32[]{:S(2)}, u32[]{:S(2)}) collective-permute-start(f32[2,384]{1,0:T(2,128)S(1)} %get-tuple-element.23), channel_id=1, source_target_pairs={{0,4},{1,5},{2,6},{3,7},{4,0},{5,1},{6,2},{7,3},{8,12},{9,13},{10,... | collective-permute-start | bytes 9224 | tf_op jit(solution)/shard_map/ppermute | solution.py:199
  23.5 0.3 local.3
  23.7 0.0 collective-permute-done.4.c0
  23.7 0.0 collective-permute-done.5.c1
  23.8 0.0 collective-permute-done.6.c2
  23.8 0.5 %collective-permute-done.7.c3 = f32[2,384]{1,0:T(2,128)S(1)} collective-permute-done((f32[2,384]{1,0:T(2,128)S(1)}, f32[2,384]{1,0:T(2,128)S(1)}, u32[]{:S(2)}, u32[]{:S(2)}) %collective-permute-start.7) | collective-permute-done | bytes 3104 | tf_op jit(solution)/shard_map/ppermute | solution.py:199
  24.3 0.8 %last.1 = (f32[2,384]{1,0:T(2,128)}, f32[16,8,128]{2,1,0:T(8,128)S(1)}) custom-call(s32[1,2]{1,0:T(1,128)S(1)} %bitcast.1, f32[2,384]{1,0:T(2,128)S(1)} %get-tuple-element.19.adjoint, f32[2,384]{1,0:T(2,128)S(1)} %copy-done.5, f32[2,384]{1,0:T(2,128)S(1)} %local.3, f32[2,384]{1,0:T(2,128)S(1)} %collective-permute-done.4.c0, ...), custom_call_target="tpu_custom_call" | custom-call | flops 884736 | bytes 884736 | tf_op jit(solution)/shard_map/last/pallas_call | solution.py:227
  25.1 12.3 %all_to_all.10.got = f32[16,8,128]{2,1,0:T(8,128)S(1)} all-to-all(f32[16,8,128]{2,1,0:T(8,128)S(1)} %get-tuple-element.25), channel_id=1, replica_groups=mesh['z'=8,'y'=4,'core'=2,'x'=4] {'z','core'}, dimensions={0} | all-to-all | bytes 131072 | tf_op jit(solution)/shard_map/all_to_all | solution.py:235
  37.4 0.2 spread.1
  37.6 10.5 %all_to_all.11.parts = f32[16,8,128]{2,1,0:T(8,128)S(1)} all-to-all(f32[16,8,128]{2,1,0:T(8,128)S(1)} %spread.1), channel_id=1, replica_groups=mesh['z'=8,'y'=4,'core'=2,'x'=4] {'y','x'}, dimensions={0} | all-to-all | bytes 131072 | tf_op jit(solution)/shard_map/all_to_all | solution.py:239
  48.1 0.6 %finish.1 = f32[1,384]{1,0:T(1,128)} custom-call(f32[1,384]{1,0:T(1,128)S(1)} %copy-done.6, f32[16,8,128]{2,1,0:T(8,128)S(1)} %all_to_all.11.parts), custom_call_target="tpu_custom_call" | custom-call | tf_op jit(solution)/shard_map/finish/pallas_call | solution.py:240
  (17 shorter events, 0.0 us)
Async XLA Ops:
  0.6 15.7 %copy-start.4 = (s32[2,5]{1,0:T(2,128)S(1)}, s32[2,5]{1,0:T(2,128)}, u32[]{:S(2)}) copy-start(s32[2,5]{1,0:T(2,128)} %names.5) | copy-start | bytes 124
  0.6 15.7 %copy-start.3 = (f32[2,384]{1,0:T(2,128)S(1)}, f32[2,384]{1,0:T(2,128)}, u32[]{:S(2)}) copy-start(f32[2,384]{1,0:T(2,128)} %adjoint.3) | copy-start | bytes 9220
  0.7 15.7 %copy-start = (bf16[2,384,384]{2,1,0:T(8,128)(2,1)S(1)}, bf16[2,384,384]{2,1,0:T(8,128)(2,1)}, u32[]{:S(2)}) copy-start(bf16[2,384,384]{2,1,0:T(8,128)(2,1)} %diag.3) | copy-start | bytes 1769476
  0.7 16.5 %copy-start.1 = (bf16[2,384,384]{2,1,0:T(8,128)(2,1)S(1)}, bf16[2,384,384]{2,1,0:T(8,128)(2,1)}, u32[]{:S(2)}) copy-start(bf16[2,384,384]{2,1,0:T(8,128)(2,1)} %precond.3) | copy-start | bytes 1769476
  0.7 16.5 %copy-start.5 = (f32[2,384]{1,0:T(2,128)S(1)}, f32[2,384]{1,0:T(2,128)}, u32[]{:S(2)}) copy-start(f32[2,384]{1,0:T(2,128)} %source.3) | copy-start | bytes 9220
  3.4 13.2 %collective-permute-start = (f32[2,384]{1,0:T(2,128)S(1)}, f32[2,384]{1,0:T(2,128)S(1)}, u32[]{:S(2)}, u32[]{:S(2)}) collective-permute-start(f32[2,384]{1,0:T(2,128)S(1)} %get-tuple-element.15), channel_id=1, source_target_pairs={{0,252},{1,253},{2,254},{3,255},{4,8},{5,9},{6,10},{7,11},{8,4},{9... | collective-permute-start | bytes 9224 | tf_op jit(solution)/shard_map/ppermute | solution.py:199
  6.2 10.5 %collective-permute-start.1 = (f32[2,384]{1,0:T(2,128)S(1)}, f32[2,384]{1,0:T(2,128)S(1)}, u32[]{:S(2)}, u32[]{:S(2)}) collective-permute-start(f32[2,384]{1,0:T(2,128)S(1)} %get-tuple-element.16), channel_id=1, source_target_pairs={{0,1},{1,0},{2,3},{3,2},{4,5},{5,4},{6,7},{7,6},{8,9},{9,8},{10,11... | collective-permute-start | bytes 9224 | tf_op jit(solution)/shard_map/ppermute | solution.py:199
  7.4 9.3 %collective-permute-start.2 = (f32[2,384]{1,0:T(2,128)S(1)}, f32[2,384]{1,0:T(2,128)S(1)}, u32[]{:S(2)}, u32[]{:S(2)}) collective-permute-start(f32[2,384]{1,0:T(2,128)S(1)} %get-tuple-element.17), channel_id=1, source_target_pairs={{0,3},{1,2},{2,1},{3,0},{4,7},{5,6},{6,5},{7,4},{8,11},{9,10},{10,... | collective-permute-start | bytes 9224 | tf_op jit(solution)/shard_map/ppermute | solution.py:199
  9.2 7.9 %collective-permute-start.3 = (f32[2,384]{1,0:T(2,128)S(1)}, f32[2,384]{1,0:T(2,128)S(1)}, u32[]{:S(2)}, u32[]{:S(2)}) collective-permute-start(f32[2,384]{1,0:T(2,128)S(1)} %get-tuple-element.18), channel_id=1, source_target_pairs={{0,4},{1,5},{2,6},{3,7},{4,0},{5,1},{6,2},{7,3},{8,12},{9,13},{10,... | collective-permute-start | bytes 9224 | tf_op jit(solution)/shard_map/ppermute | solution.py:199
  16.6 7.6 %copy-start.2 = (bf16[384,384]{1,0:T(8,128)(2,1)S(1)}, bf16[384,384]{1,0:T(8,128)(2,1)}, u32[]{:S(2)}) copy-start(bf16[384,384]{1,0:T(8,128)(2,1)} %surf.1) | copy-start | bytes 884740
  16.6 7.6 %copy-start.7 = (s32[2]{0:T(128)S(1)}, s32[2]{0:T(128)}, u32[]{:S(2)}) copy-start(s32[2]{0:T(128)} %param.16) | copy-start | bytes 28
  17.8 30.3 %copy-start.6 = (f32[1,384]{1,0:T(1,128)S(1)}, f32[1,384]{1,0:T(1,128)}, u32[]{:S(2)}) copy-start(f32[1,384]{1,0:T(1,128)} %grad.1) | copy-start | bytes 4612
  17.8 5.9 %collective-permute-start.4 = (f32[2,384]{1,0:T(2,128)S(1)}, f32[2,384]{1,0:T(2,128)S(1)}, u32[]{:S(2)}, u32[]{:S(2)}) collective-permute-start(f32[2,384]{1,0:T(2,128)S(1)} %get-tuple-element.20), channel_id=1, source_target_pairs={{0,252},{1,253},{2,254},{3,255},{4,8},{5,9},{6,10},{7,11},{8,4},{9... | collective-permute-start | bytes 9224 | tf_op jit(solution)/shard_map/ppermute | solution.py:199
  17.9 5.8 %collective-permute-start.5 = (f32[2,384]{1,0:T(2,128)S(1)}, f32[2,384]{1,0:T(2,128)S(1)}, u32[]{:S(2)}, u32[]{:S(2)}) collective-permute-start(f32[2,384]{1,0:T(2,128)S(1)} %get-tuple-element.21), channel_id=1, source_target_pairs={{0,1},{1,0},{2,3},{3,2},{4,5},{5,4},{6,7},{7,6},{8,9},{9,8},{10,11... | collective-permute-start | bytes 9224 | tf_op jit(solution)/shard_map/ppermute | solution.py:199
  18.3 5.4 %collective-permute-start.6 = (f32[2,384]{1,0:T(2,128)S(1)}, f32[2,384]{1,0:T(2,128)S(1)}, u32[]{:S(2)}, u32[]{:S(2)}) collective-permute-start(f32[2,384]{1,0:T(2,128)S(1)} %get-tuple-element.22), channel_id=1, source_target_pairs={{0,3},{1,2},{2,1},{3,0},{4,7},{5,6},{6,5},{7,4},{8,11},{9,10},{10,... | collective-permute-start | bytes 9224 | tf_op jit(solution)/shard_map/ppermute | solution.py:199
  19.0 5.3 %collective-permute-start.7 = (f32[2,384]{1,0:T(2,128)S(1)}, f32[2,384]{1,0:T(2,128)S(1)}, u32[]{:S(2)}, u32[]{:S(2)}) collective-permute-start(f32[2,384]{1,0:T(2,128)S(1)} %get-tuple-element.23), channel_id=1, source_target_pairs={{0,4},{1,5},{2,6},{3,7},{4,0},{5,1},{6,2},{7,3},{8,12},{9,13},{10,... | collective-permute-start | bytes 9224 | tf_op jit(solution)/shard_map/ppermute | solution.py:199

commit v4 on v3

--- a/solution.py
+++ b/solution.py
@@ -71,33 +71,46 @@
         out[...] = total
 
 
-def first_kernel(names_in, adjoint_in, off_in, c0, c1, c2, c3, off, names, adjoint, sems):
+def first_kernel(names_in, adjoint_in, off_in, c0, c1, c2, c3, off, names, adjoint, left, sums, sems):
     slots = [jnp.where(which == 0, even, odd) for even, odd, which in message_slots()]
+    count = adjoint.shape[0]
     heads = [
         pltpu.make_async_copy(names_in, names, sems.at[5]),
         pltpu.make_async_copy(adjoint_in, adjoint, sems.at[6]),
     ]
-    blocks = [
-        pltpu.make_async_copy(off_in.at[:, slot], off.at[:, slot], sems.at[m])
-        for m, slot in enumerate(slots + [0])
-    ]
-    for copy in heads + blocks:
+
+    def block(m):
+        slot = sum(jnp.where(m == i, slots[i], 0) for i in range(len(slots)))
+        return slot, pltpu.make_async_copy(off_in.at[:, slot], off.at[:, slot], sems.at[m])
+
+    for copy in heads:
         copy.start()
+
+    @pl.loop(0, len(slots) + 1)
+    def _(m):
+        block(m)[1].start()
+
     for copy in heads:
         copy.wait()
-
-    def arrived(m, slot):
-        def block(row):
-            if row == 0:
-                blocks[m].wait()
-            return off[row, slot]
-
-        return block
-
-    send_all(
-        adjoint[...], names, [arrived(m, slot) for m, slot in enumerate(slots)], (c0, c1, c2, c3)
-    )
-    blocks[-1].wait()
+    for m, (even, odd, which) in enumerate(message_slots()):
+        for row in range(count):
+            here = slice(row, row + 1)
+            name = jnp.where(which == 0, names[here, even : even + 1], names[here, odd : odd + 1])
+            left[m, row] = placed(adjoint[here, :], count, name % count)
+
+    @pl.loop(0, len(slots))
+    def _(m):
+        slot, copy = block(m)
+        copy.wait()
+        sums[m] = jnp.zeros(sums.shape[1:], F32)
+
+        @pl.loop(0, count)
+        def _(row):
+            sums[m] += matmul(left[m, row], off[row, slot])
+
+    for m, out in enumerate((c0, c1, c2, c3)):
+        out[...] = sums[m]
+    block(len(slots))[1].wait()
 
 
 def local_kernel(names, adjoint, off, diag, out):
@@ -167,7 +180,8 @@
         out[:, i, :] = jnp.zeros((group, LANES), F32)
 
 
-def finish_kernel(grad, parts, out):
+def finish_kernel(grad, parts, values, adjoint, out):
+    adjoint[...] = values[...]
     total = jnp.sum(parts[...], axis=0)
     for i in range(grad.shape[1] // LANES):
         where = slice(i * LANES, (i + 1) * LANES)
@@ -209,6 +223,8 @@
         [
             pltpu.VMEM(neighbours.shape, jnp.int32),
             pltpu.VMEM((count, width), F32),
+            pltpu.VMEM((4, count, count, width), BF16),
+            pltpu.VMEM((4, count, width), F32),
             pltpu.SemaphoreType.DMA((7,)),
         ],
         52,
@@ -227,7 +243,7 @@
     adjoint, payload = call(
         last_kernel,
         [VMEM] * 10,
-        [block, jax.ShapeDtypeStruct((plane, 8, LANES), F32)],
+        [pltpu.VMEM((count, width), F32), pltpu.VMEM((plane, 8, LANES), F32)],
         "last",
         6 * matrix,
         6 * matrix,
@@ -237,9 +253,12 @@
         spread_kernel, [VMEM], [jax.ShapeDtypeStruct((line, 8, LANES), F32)], "spread"
     )(got)
     parts = lax.all_to_all(sums, SECOND, 0, 0, tiled=True)
-    (sensitivity,) = call(
-        finish_kernel, [VMEM, VMEM], [jax.ShapeDtypeStruct((1, width), F32)], "finish"
-    )(surface_grad, parts)
+    adjoint, sensitivity = call(
+        finish_kernel,
+        [VMEM] * 3,
+        [jax.ShapeDtypeStruct((count, width), F32), jax.ShapeDtypeStruct((1, width), F32)],
+        "finish",
+    )(surface_grad, parts, adjoint)
     return (adjoint, sensitivity)
 
 

time: 48.8 us -> 48.3 us (0.990)
  Pallas kernels: 5.56 us -> 5.02 us
where the time goes in v4:
time: 48.3 us; the launch traced here: 48.2 us
  blocking collectives  22.8 us (47%)
  starting transfers between devices  18.5 us (38%)
  Pallas kernels  5.02 us (10%)
  waiting for transfers between devices  1.02 us (2%)
  between operations  0.76 us (2%)
    ppermute x8, starting transfers between devices, swap(): lax.ppermute(m, ALL, route)  18.5 us
    all_to_all x1, blocking collectives, on_device(): got = lax.all_to_all(payload, FIRST, 0, 0, tiled=True)  12.3 us
    all_to_all x1, blocking collectives, on_device(): parts = lax.all_to_all(sums, SECOND, 0, 0, tiled=True)  10.5 us
    pallas_call x1, Pallas kernels, on_device(): call(first_kernel, [HBM] * 3, [pltpu.VMEM((count, width), F32)] * 4 + [pl...  2.63 us
    ppermute x8, waiting for transfers between devices, swap(): lax.ppermute(m, ALL, route)  1.02 us
  transfers between devices with their start and end apart: 8, of which 2 were waited for; matrix products, arithmetic and copies ran while one was open for 0% of the time, Pallas kernels for 1%

profile of v4, /device:TPU:1, one launch (start us, length us, event | category | flops | bytes accessed | tf_op | source)
XLA Modules:
  0.0 48.2 jit_solution(11956996022304860976)
XLA Ops:
  0.7 2.6 %first.1 = (f32[2,384]{1,0:T(2,128)S(1)}, f32[2,384]{1,0:T(2,128)S(1)}, f32[2,384]{1,0:T(2,128)S(1)}, f32[2,384]{1,0:T(2,128)S(1)}, bf16[2,5,384,384]{3,2,1,0:T(8,128)(2,1)S(1)}) custom-call(s32[2,5]{1,0:T(2,128)} %names.5, f32[2,384]{1,0:T(2,128)} %adjoint.3, bf16[2,5,384,384]{3,2,1,0:T(8,128)(2,1)} %off_in.1), custom_call_target="tpu_custom_call" | custom-call | flops 2359296 | bytes 2359296 | tf_op jit(solution)/shard_map/first/pallas_call | solution.py:216
  3.3 2.8 %collective-permute-start = (f32[2,384]{1,0:T(2,128)S(1)}, f32[2,384]{1,0:T(2,128)S(1)}, u32[]{:S(2)}, u32[]{:S(2)}) collective-permute-start(f32[2,384]{1,0:T(2,128)S(1)} %get-tuple-element.15), channel_id=1, source_target_pairs={{0,252},{1,253},{2,254},{3,255},{4,8},{5,9},{6,10},{7,11},{8,4},{9... | collective-permute-start | bytes 9224 | tf_op jit(solution)/shard_map/ppermute | solution.py:213
  6.1 1.2 %collective-permute-start.1 = (f32[2,384]{1,0:T(2,128)S(1)}, f32[2,384]{1,0:T(2,128)S(1)}, u32[]{:S(2)}, u32[]{:S(2)}) collective-permute-start(f32[2,384]{1,0:T(2,128)S(1)} %get-tuple-element.16), channel_id=1, source_target_pairs={{0,1},{1,0},{2,3},{3,2},{4,5},{5,4},{6,7},{7,6},{8,9},{9,8},{10,11... | collective-permute-start | bytes 9224 | tf_op jit(solution)/shard_map/ppermute | solution.py:213
  7.3 1.8 %collective-permute-start.2 = (f32[2,384]{1,0:T(2,128)S(1)}, f32[2,384]{1,0:T(2,128)S(1)}, u32[]{:S(2)}, u32[]{:S(2)}) collective-permute-start(f32[2,384]{1,0:T(2,128)S(1)} %get-tuple-element.17), channel_id=1, source_target_pairs={{0,3},{1,2},{2,1},{3,0},{4,7},{5,6},{6,5},{7,4},{8,11},{9,10},{10,... | collective-permute-start | bytes 9224 | tf_op jit(solution)/shard_map/ppermute | solution.py:213
  9.1 7.1 %collective-permute-start.3 = (f32[2,384]{1,0:T(2,128)S(1)}, f32[2,384]{1,0:T(2,128)S(1)}, u32[]{:S(2)}, u32[]{:S(2)}) collective-permute-start(f32[2,384]{1,0:T(2,128)S(1)} %get-tuple-element.18), channel_id=1, source_target_pairs={{0,4},{1,5},{2,6},{3,7},{4,0},{5,1},{6,2},{7,3},{8,12},{9,13},{10,... | collective-permute-start | bytes 9224 | tf_op jit(solution)/shard_map/ppermute | solution.py:213
  16.3 0.3 local.2
  16.5 0.0 collective-permute-done.c0
  16.6 0.0 collective-permute-done.1.c1
  16.6 0.5 %collective-permute-done.3.c3 = f32[2,384]{1,0:T(2,128)S(1)} collective-permute-done((f32[2,384]{1,0:T(2,128)S(1)}, f32[2,384]{1,0:T(2,128)S(1)}, u32[]{:S(2)}, u32[]{:S(2)}) %collective-permute-start.3) | collective-permute-done | bytes 3104 | tf_op jit(solution)/shard_map/ppermute | solution.py:213
  17.1 0.7 %middle.1 = (f32[2,384]{1,0:T(2,128)S(1)}, f32[2,384]{1,0:T(2,128)S(1)}, f32[2,384]{1,0:T(2,128)S(1)}, f32[2,384]{1,0:T(2,128)S(1)}, f32[2,384]{1,0:T(2,128)S(1)}) custom-call(s32[2,5]{1,0:T(2,128)S(1)} %copy-done.4, f32[2,384]{1,0:T(2,128)S(1)} %copy-done.3, f32[2,384]{1,0:T(2,128)S(1)} %copy-done.5, f32[2,384]{1,0:T(2,128)S(1)} %local.2, ...), custom_call_target="tpu_custom_call" | custom-call | flops 2949120 | bytes 2949120 | tf_op jit(solution)/shard_map/middle/pallas_call | solution.py:235
  17.7 0.1 collective-permute-start.4
  17.8 0.4 collective-permute-start.5
  18.2 0.6 %collective-permute-start.6 = (f32[2,384]{1,0:T(2,128)S(1)}, f32[2,384]{1,0:T(2,128)S(1)}, u32[]{:S(2)}, u32[]{:S(2)}) collective-permute-start(f32[2,384]{1,0:T(2,128)S(1)} %get-tuple-element.22), channel_id=1, source_target_pairs={{0,3},{1,2},{2,1},{3,0},{4,7},{5,6},{6,5},{7,4},{8,11},{9,10},{10,... | collective-permute-start | bytes 9224 | tf_op jit(solution)/shard_map/ppermute | solution.py:213
  18.9 4.5 %collective-permute-start.7 = (f32[2,384]{1,0:T(2,128)S(1)}, f32[2,384]{1,0:T(2,128)S(1)}, u32[]{:S(2)}, u32[]{:S(2)}) collective-permute-start(f32[2,384]{1,0:T(2,128)S(1)} %get-tuple-element.23), channel_id=1, source_target_pairs={{0,4},{1,5},{2,6},{3,7},{4,0},{5,1},{6,2},{7,3},{8,12},{9,13},{10,... | collective-permute-start | bytes 9224 | tf_op jit(solution)/shard_map/ppermute | solution.py:213
  23.4 0.3 local.3
  23.6 0.0 collective-permute-done.4.c0
  23.7 0.0 collective-permute-done.5.c1
  23.7 0.0 collective-permute-done.6.c2
  23.7 0.5 %collective-permute-done.7.c3 = f32[2,384]{1,0:T(2,128)S(1)} collective-permute-done((f32[2,384]{1,0:T(2,128)S(1)}, f32[2,384]{1,0:T(2,128)S(1)}, u32[]{:S(2)}, u32[]{:S(2)}) %collective-permute-start.7) | collective-permute-done | bytes 3104 | tf_op jit(solution)/shard_map/ppermute | solution.py:213
  24.2 0.3 last.1
  24.5 12.3 %all_to_all.10.got = f32[16,8,128]{2,1,0:T(8,128)S(1)} all-to-all(f32[16,8,128]{2,1,0:T(8,128)S(1)} %get-tuple-element.24), channel_id=1, replica_groups=mesh['z'=8,'y'=4,'core'=2,'x'=4] {'z','core'}, dimensions={0} | all-to-all | bytes 131072 | tf_op jit(solution)/shard_map/all_to_all | solution.py:251
  36.9 0.2 spread.1
  37.1 10.5 %all_to_all.11.parts = f32[16,8,128]{2,1,0:T(8,128)S(1)} all-to-all(f32[16,8,128]{2,1,0:T(8,128)S(1)} %spread.1), channel_id=1, replica_groups=mesh['z'=8,'y'=4,'core'=2,'x'=4] {'y','x'}, dimensions={0} | all-to-all | bytes 131072 | tf_op jit(solution)/shard_map/all_to_all | solution.py:255
  47.6 0.6 %finish.1 = (f32[2,384]{1,0:T(2,128)}, f32[1,384]{1,0:T(1,128)}) custom-call(f32[1,384]{1,0:T(1,128)S(1)} %copy-done.6, f32[16,8,128]{2,1,0:T(8,128)S(1)} %all_to_all.11.parts, f32[2,384]{1,0:T(2,128)S(1)} %get-tuple-element.25.values), custom_call_target="tpu_custom_call" | custom-call | tf_op jit(solution)/shard_map/finish/pallas_call | solution.py:256
  (17 shorter events, 0.0 us)
Async XLA Ops:
  0.6 15.6 %copy-start.4 = (s32[2,5]{1,0:T(2,128)S(1)}, s32[2,5]{1,0:T(2,128)}, u32[]{:S(2)}) copy-start(s32[2,5]{1,0:T(2,128)} %names.5) | copy-start | bytes 124
  0.6 15.6 %copy-start.3 = (f32[2,384]{1,0:T(2,128)S(1)}, f32[2,384]{1,0:T(2,128)}, u32[]{:S(2)}) copy-start(f32[2,384]{1,0:T(2,128)} %adjoint.3) | copy-start | bytes 9220
  0.7 15.6 %copy-start = (bf16[2,384,384]{2,1,0:T(8,128)(2,1)S(1)}, bf16[2,384,384]{2,1,0:T(8,128)(2,1)}, u32[]{:S(2)}) copy-start(bf16[2,384,384]{2,1,0:T(8,128)(2,1)} %diag.3) | copy-start | bytes 1769476
  0.7 16.4 %copy-start.1 = (bf16[2,384,384]{2,1,0:T(8,128)(2,1)S(1)}, bf16[2,384,384]{2,1,0:T(8,128)(2,1)}, u32[]{:S(2)}) copy-start(bf16[2,384,384]{2,1,0:T(8,128)(2,1)} %precond.3) | copy-start | bytes 1769476
  0.7 16.4 %copy-start.5 = (f32[2,384]{1,0:T(2,128)S(1)}, f32[2,384]{1,0:T(2,128)}, u32[]{:S(2)}) copy-start(f32[2,384]{1,0:T(2,128)} %source.3) | copy-start | bytes 9220
  3.3 13.2 %collective-permute-start = (f32[2,384]{1,0:T(2,128)S(1)}, f32[2,384]{1,0:T(2,128)S(1)}, u32[]{:S(2)}, u32[]{:S(2)}) collective-permute-start(f32[2,384]{1,0:T(2,128)S(1)} %get-tuple-element.15), channel_id=1, source_target_pairs={{0,252},{1,253},{2,254},{3,255},{4,8},{5,9},{6,10},{7,11},{8,4},{9... | collective-permute-start | bytes 9224 | tf_op jit(solution)/shard_map/ppermute | solution.py:213
  6.1 10.5 %collective-permute-start.1 = (f32[2,384]{1,0:T(2,128)S(1)}, f32[2,384]{1,0:T(2,128)S(1)}, u32[]{:S(2)}, u32[]{:S(2)}) collective-permute-start(f32[2,384]{1,0:T(2,128)S(1)} %get-tuple-element.16), channel_id=1, source_target_pairs={{0,1},{1,0},{2,3},{3,2},{4,5},{5,4},{6,7},{7,6},{8,9},{9,8},{10,11... | collective-permute-start | bytes 9224 | tf_op jit(solution)/shard_map/ppermute | solution.py:213
  7.3 9.3 %collective-permute-start.2 = (f32[2,384]{1,0:T(2,128)S(1)}, f32[2,384]{1,0:T(2,128)S(1)}, u32[]{:S(2)}, u32[]{:S(2)}) collective-permute-start(f32[2,384]{1,0:T(2,128)S(1)} %get-tuple-element.17), channel_id=1, source_target_pairs={{0,3},{1,2},{2,1},{3,0},{4,7},{5,6},{6,5},{7,4},{8,11},{9,10},{10,... | collective-permute-start | bytes 9224 | tf_op jit(solution)/shard_map/ppermute | solution.py:213
  9.1 7.9 %collective-permute-start.3 = (f32[2,384]{1,0:T(2,128)S(1)}, f32[2,384]{1,0:T(2,128)S(1)}, u32[]{:S(2)}, u32[]{:S(2)}) collective-permute-start(f32[2,384]{1,0:T(2,128)S(1)} %get-tuple-element.18), channel_id=1, source_target_pairs={{0,4},{1,5},{2,6},{3,7},{4,0},{5,1},{6,2},{7,3},{8,12},{9,13},{10,... | collective-permute-start | bytes 9224 | tf_op jit(solution)/shard_map/ppermute | solution.py:213
  16.5 7.6 %copy-start.2 = (bf16[384,384]{1,0:T(8,128)(2,1)S(1)}, bf16[384,384]{1,0:T(8,128)(2,1)}, u32[]{:S(2)}) copy-start(bf16[384,384]{1,0:T(8,128)(2,1)} %surf.1) | copy-start | bytes 884740
  16.5 7.6 %copy-start.7 = (s32[2]{0:T(128)S(1)}, s32[2]{0:T(128)}, u32[]{:S(2)}) copy-start(s32[2]{0:T(128)} %param.16) | copy-start | bytes 28
  17.7 29.8 %copy-start.6 = (f32[1,384]{1,0:T(1,128)S(1)}, f32[1,384]{1,0:T(1,128)}, u32[]{:S(2)}) copy-start(f32[1,384]{1,0:T(1,128)} %grad.1) | copy-start | bytes 4612
  17.7 5.9 %collective-permute-start.4 = (f32[2,384]{1,0:T(2,128)S(1)}, f32[2,384]{1,0:T(2,128)S(1)}, u32[]{:S(2)}, u32[]{:S(2)}) collective-permute-start(f32[2,384]{1,0:T(2,128)S(1)} %get-tuple-element.20), channel_id=1, source_target_pairs={{0,252},{1,253},{2,254},{3,255},{4,8},{5,9},{6,10},{7,11},{8,4},{9... | collective-permute-start | bytes 9224 | tf_op jit(solution)/shard_map/ppermute | solution.py:213
  17.8 5.8 %collective-permute-start.5 = (f32[2,384]{1,0:T(2,128)S(1)}, f32[2,384]{1,0:T(2,128)S(1)}, u32[]{:S(2)}, u32[]{:S(2)}) collective-permute-start(f32[2,384]{1,0:T(2,128)S(1)} %get-tuple-element.21), channel_id=1, source_target_pairs={{0,1},{1,0},{2,3},{3,2},{4,5},{5,4},{6,7},{7,6},{8,9},{9,8},{10,11... | collective-permute-start | bytes 9224 | tf_op jit(solution)/shard_map/ppermute | solution.py:213
  18.2 5.4 %collective-permute-start.6 = (f32[2,384]{1,0:T(2,128)S(1)}, f32[2,384]{1,0:T(2,128)S(1)}, u32[]{:S(2)}, u32[]{:S(2)}) collective-permute-start(f32[2,384]{1,0:T(2,128)S(1)} %get-tuple-element.22), channel_id=1, source_target_pairs={{0,3},{1,2},{2,1},{3,0},{4,7},{5,6},{6,5},{7,4},{8,11},{9,10},{10,... | collective-permute-start | bytes 9224 | tf_op jit(solution)/shard_map/ppermute | solution.py:213
  18.9 5.3 %collective-permute-start.7 = (f32[2,384]{1,0:T(2,128)S(1)}, f32[2,384]{1,0:T(2,128)S(1)}, u32[]{:S(2)}, u32[]{:S(2)}) collective-permute-start(f32[2,384]{1,0:T(2,128)S(1)} %get-tuple-element.23), channel_id=1, source_target_pairs={{0,4},{1,5},{2,6},{3,7},{4,0},{5,1},{6,2},{7,3},{8,12},{9,13},{10,... | collective-permute-start | bytes 9224 | tf_op jit(solution)/shard_map/ppermute | solution.py:213

commit v5 on v4

--- a/solution.py
+++ b/solution.py
@@ -10,8 +10,8 @@
 CUT = {"z": 8, "y": 4, "core": 2, "x": 4}
 ALL = tuple(CUT)
 LANES = 128
-FIRST, SECOND = ('z', 'core'), ('y', 'x')
-ORDER = (3, 1, 2, 0)
+FIRST, SECOND = (('core', 'z'), ('y', 'x'))
+ORDERS = ((3, 2, 1, 0), (3, 1, 2, 0))
 F32 = jnp.float32
 BF16 = jnp.bfloat16
 VMEM = pl.BlockSpec(memory_space=pltpu.VMEM)
@@ -42,10 +42,10 @@
     return jnp.dot(left, right, preferred_element_type=F32)
 
 
-def message_slots():
+def message_slots(sweep):
     core, odd = lax.axis_index("core"), lax.axis_index("x") % 2
     four = (1, 2, core), (3, 4, odd), (4, 3, odd), (2, 1, core)
-    return [four[i] for i in ORDER]
+    return [four[i] for i in ORDERS[sweep]]
 
 
 def step(adjoint, source, local, came, precond_ref):
@@ -61,7 +61,7 @@
 
 def send_all(values, names, off, outs):
     count = values.shape[0]
-    for (even, odd, which), out, blocks in zip(message_slots(), outs, off, strict=True):
+    for (even, odd, which), out, blocks in zip(message_slots(1), outs, off, strict=True):
         total = jnp.zeros(out.shape, F32)
         for row in range(count):
             here = slice(row, row + 1)
@@ -72,7 +72,7 @@
 
 
 def first_kernel(names_in, adjoint_in, off_in, c0, c1, c2, c3, off, names, adjoint, left, sums, sems):
-    slots = [jnp.where(which == 0, even, odd) for even, odd, which in message_slots()]
+    slots = [jnp.where(which == 0, even, odd) for even, odd, which in message_slots(0)]
     count = adjoint.shape[0]
     heads = [
         pltpu.make_async_copy(names_in, names, sems.at[5]),
@@ -92,7 +92,7 @@
 
     for copy in heads:
         copy.wait()
-    for m, (even, odd, which) in enumerate(message_slots()):
+    for m, (even, odd, which) in enumerate(message_slots(0)):
         for row in range(count):
             here = slice(row, row + 1)
             name = jnp.where(which == 0, names[here, even : even + 1], names[here, odd : odd + 1])
@@ -126,7 +126,7 @@
 def middle_kernel(names, adjoint, source, local, c0, c1, c2, c3, precond, off, new, *outs):
     values = step(adjoint[...], source[...], local[...], (c0, c1, c2, c3), precond)
     new[...] = values
-    slots = [jnp.where(which == 0, even, odd) for even, odd, which in message_slots()]
+    slots = [jnp.where(which == 0, even, odd) for even, odd, which in message_slots(1)]
     send_all(values, names, [lambda row, slot=slot: off[row, slot] for slot in slots], outs)
 
 
@@ -206,11 +206,11 @@
 ):
     count, width = adjoint_start.shape
     routes = [pairs("dom", 0), pairs("sub", 0), pairs("sub", 1), pairs("dom", 1)]
-    routes = [routes[i] for i in ORDER]
     block = jax.ShapeDtypeStruct((count, width), F32)
 
-    def swap(messages):
-        return [lax.ppermute(m, ALL, route) for m, route in zip(messages, routes, strict=True)]
+    def swap(messages, sweep):
+        order = [routes[i] for i in ORDERS[sweep]]
+        return [lax.ppermute(m, ALL, route) for m, route in zip(messages, order, strict=True)]
 
     matrix = width * width
     *messages, off = call(
@@ -229,13 +229,13 @@
         ],
         52,
     )(neighbours, adjoint_start, jac_off)
-    came = swap(messages)
+    came = swap(messages, 0)
     local_call = call(local_kernel, [VMEM] * 4, [block], "local", 8 * matrix, 8 * matrix)
     (local,) = local_call(neighbours, adjoint_start, off, jac_diag)
     adjoint, *messages = call(
         middle_kernel, [VMEM] * 10, [block] * 5, "middle", 20 * matrix, 20 * matrix
     )(neighbours, adjoint_start, source, local, *came, precond, off)
-    came = swap(messages)
+    came = swap(messages, 1)
     (local,) = local_call(neighbours, adjoint, off, jac_diag)
 
     plane = math.prod(CUT[axis] for axis in FIRST)

time: 48.3 us -> 46.9 us (0.971)
  blocking collectives: 22.8 us -> 21.4 us
    all_to_all x1, blocking collectives: 10.5 us -> 9.17 us  [on_device(): parts = lax.all_to_all(sums, SECOND, 0, 0, tiled=True)]
where the time goes in v5:
time: 46.9 us; the launch traced here: 46.7 us
  blocking collectives  21.4 us (46%)
  starting transfers between devices  18.5 us (39%)
  Pallas kernels  5.03 us (11%)
  waiting for transfers between devices  1.02 us (2%)
  between operations  0.75 us (2%)
    ppermute x8, starting transfers between devices, swap(): lax.ppermute(m, ALL, route)  18.5 us
    all_to_all x1, blocking collectives, on_device(): got = lax.all_to_all(payload, FIRST, 0, 0, tiled=True)  12.2 us
    all_to_all x1, blocking collectives, on_device(): parts = lax.all_to_all(sums, SECOND, 0, 0, tiled=True)  9.17 us
    pallas_call x1, Pallas kernels, on_device(): call(first_kernel, [HBM] * 3, [pltpu.VMEM((count, width), F32)] * 4 + [pl...  2.63 us
    ppermute x8, waiting for transfers between devices, swap(): lax.ppermute(m, ALL, route)  1.02 us
  transfers between devices with their start and end apart: 8, of which 2 were waited for; matrix products, arithmetic and copies ran while one was open for 0% of the time, Pallas kernels for 1%

profile of v5, /device:TPU:1, one launch (start us, length us, event | category | flops | bytes accessed | tf_op | source)
XLA Modules:
  0.0 46.7 jit_solution(14988187077649481694)
XLA Ops:
  0.7 2.6 %first.1 = (f32[2,384]{1,0:T(2,128)S(1)}, f32[2,384]{1,0:T(2,128)S(1)}, f32[2,384]{1,0:T(2,128)S(1)}, f32[2,384]{1,0:T(2,128)S(1)}, bf16[2,5,384,384]{3,2,1,0:T(8,128)(2,1)S(1)}) custom-call(s32[2,5]{1,0:T(2,128)} %names.5, f32[2,384]{1,0:T(2,128)} %adjoint.3, bf16[2,5,384,384]{3,2,1,0:T(8,128)(2,1)} %off_in.1), custom_call_target="tpu_custom_call" | custom-call | flops 2359296 | bytes 2359296 | tf_op jit(solution)/shard_map/first/pallas_call | solution.py:216
  3.3 2.8 %collective-permute-start = (f32[2,384]{1,0:T(2,128)S(1)}, f32[2,384]{1,0:T(2,128)S(1)}, u32[]{:S(2)}, u32[]{:S(2)}) collective-permute-start(f32[2,384]{1,0:T(2,128)S(1)} %get-tuple-element.15), channel_id=1, source_target_pairs={{0,252},{1,253},{2,254},{3,255},{4,8},{5,9},{6,10},{7,11},{8,4},{9... | collective-permute-start | bytes 9224 | tf_op jit(solution)/shard_map/ppermute | solution.py:213
  6.1 2.5 %collective-permute-start.1 = (f32[2,384]{1,0:T(2,128)S(1)}, f32[2,384]{1,0:T(2,128)S(1)}, u32[]{:S(2)}, u32[]{:S(2)}) collective-permute-start(f32[2,384]{1,0:T(2,128)S(1)} %get-tuple-element.16), channel_id=1, source_target_pairs={{0,3},{1,2},{2,1},{3,0},{4,7},{5,6},{6,5},{7,4},{8,11},{9,10},{10,... | collective-permute-start | bytes 9224 | tf_op jit(solution)/shard_map/ppermute | solution.py:213
  8.6 0.0 collective-permute-start.2
  8.6 7.1 %collective-permute-start.3 = (f32[2,384]{1,0:T(2,128)S(1)}, f32[2,384]{1,0:T(2,128)S(1)}, u32[]{:S(2)}, u32[]{:S(2)}) collective-permute-start(f32[2,384]{1,0:T(2,128)S(1)} %get-tuple-element.18), channel_id=1, source_target_pairs={{0,4},{1,5},{2,6},{3,7},{4,0},{5,1},{6,2},{7,3},{8,12},{9,13},{10,... | collective-permute-start | bytes 9224 | tf_op jit(solution)/shard_map/ppermute | solution.py:213
  15.6 0.3 local.2
  15.9 0.0 collective-permute-done.c0
  16.0 0.0 collective-permute-done.2.c2
  16.0 0.5 %collective-permute-done.3.c3 = f32[2,384]{1,0:T(2,128)S(1)} collective-permute-done((f32[2,384]{1,0:T(2,128)S(1)}, f32[2,384]{1,0:T(2,128)S(1)}, u32[]{:S(2)}, u32[]{:S(2)}) %collective-permute-start.3) | collective-permute-done | bytes 3104 | tf_op jit(solution)/shard_map/ppermute | solution.py:213
  16.5 0.7 %middle.1 = (f32[2,384]{1,0:T(2,128)S(1)}, f32[2,384]{1,0:T(2,128)S(1)}, f32[2,384]{1,0:T(2,128)S(1)}, f32[2,384]{1,0:T(2,128)S(1)}, f32[2,384]{1,0:T(2,128)S(1)}) custom-call(s32[2,5]{1,0:T(2,128)S(1)} %copy-done.4, f32[2,384]{1,0:T(2,128)S(1)} %copy-done.3, f32[2,384]{1,0:T(2,128)S(1)} %copy-done.5, f32[2,384]{1,0:T(2,128)S(1)} %local.2, ...), custom_call_target="tpu_custom_call" | custom-call | flops 2949120 | bytes 2949120 | tf_op jit(solution)/shard_map/middle/pallas_call | solution.py:235
  17.1 0.1 collective-permute-start.4
  17.2 1.6 %collective-permute-start.5 = (f32[2,384]{1,0:T(2,128)S(1)}, f32[2,384]{1,0:T(2,128)S(1)}, u32[]{:S(2)}, u32[]{:S(2)}) collective-permute-start(f32[2,384]{1,0:T(2,128)S(1)} %get-tuple-element.21), channel_id=1, source_target_pairs={{0,1},{1,0},{2,3},{3,2},{4,5},{5,4},{6,7},{7,6},{8,9},{9,8},{10,11... | collective-permute-start | bytes 9224 | tf_op jit(solution)/shard_map/ppermute | solution.py:213
  18.8 0.2 collective-permute-start.6
  19.0 4.3 %collective-permute-start.7 = (f32[2,384]{1,0:T(2,128)S(1)}, f32[2,384]{1,0:T(2,128)S(1)}, u32[]{:S(2)}, u32[]{:S(2)}) collective-permute-start(f32[2,384]{1,0:T(2,128)S(1)} %get-tuple-element.23), channel_id=1, source_target_pairs={{0,4},{1,5},{2,6},{3,7},{4,0},{5,1},{6,2},{7,3},{8,12},{9,13},{10,... | collective-permute-start | bytes 9224 | tf_op jit(solution)/shard_map/ppermute | solution.py:213
  23.4 0.3 local.3
  23.6 0.0 collective-permute-done.4.c0
  23.7 0.0 collective-permute-done.5.c1
  23.7 0.0 collective-permute-done.6.c2
  23.7 0.5 %collective-permute-done.7.c3 = f32[2,384]{1,0:T(2,128)S(1)} collective-permute-done((f32[2,384]{1,0:T(2,128)S(1)}, f32[2,384]{1,0:T(2,128)S(1)}, u32[]{:S(2)}, u32[]{:S(2)}) %collective-permute-start.7) | collective-permute-done | bytes 3104 | tf_op jit(solution)/shard_map/ppermute | solution.py:213
  24.2 0.3 last.1
  24.5 12.2 %all_to_all.10.got = f32[16,8,128]{2,1,0:T(8,128)S(1)} all-to-all(f32[16,8,128]{2,1,0:T(8,128)S(1)} %get-tuple-element.24), channel_id=1, replica_groups=mesh['z'=8,'y'=4,'core'=2,'x'=4] {'core','z'}, dimensions={0} | all-to-all | bytes 131072 | tf_op jit(solution)/shard_map/all_to_all | solution.py:251
  36.7 0.2 spread.1
  37.0 9.2 %all_to_all.11.parts = f32[16,8,128]{2,1,0:T(8,128)S(1)} all-to-all(f32[16,8,128]{2,1,0:T(8,128)S(1)} %spread.1), channel_id=1, replica_groups=mesh['z'=8,'y'=4,'core'=2,'x'=4] {'y','x'}, dimensions={0} | all-to-all | bytes 131072 | tf_op jit(solution)/shard_map/all_to_all | solution.py:255
  46.1 0.6 %finish.1 = (f32[2,384]{1,0:T(2,128)}, f32[1,384]{1,0:T(1,128)}) custom-call(f32[1,384]{1,0:T(1,128)S(1)} %copy-done.6, f32[16,8,128]{2,1,0:T(8,128)S(1)} %all_to_all.11.parts, f32[2,384]{1,0:T(2,128)S(1)} %get-tuple-element.25.values), custom_call_target="tpu_custom_call" | custom-call | tf_op jit(solution)/shard_map/finish/pallas_call | solution.py:256
  (17 shorter events, 0.0 us)
Async XLA Ops:
  0.6 15.0 %copy-start.4 = (s32[2,5]{1,0:T(2,128)S(1)}, s32[2,5]{1,0:T(2,128)}, u32[]{:S(2)}) copy-start(s32[2,5]{1,0:T(2,128)} %names.5) | copy-start | bytes 124
  0.6 15.0 %copy-start.3 = (f32[2,384]{1,0:T(2,128)S(1)}, f32[2,384]{1,0:T(2,128)}, u32[]{:S(2)}) copy-start(f32[2,384]{1,0:T(2,128)} %adjoint.3) | copy-start | bytes 9220
  0.7 15.0 %copy-start = (bf16[2,384,384]{2,1,0:T(8,128)(2,1)S(1)}, bf16[2,384,384]{2,1,0:T(8,128)(2,1)}, u32[]{:S(2)}) copy-start(bf16[2,384,384]{2,1,0:T(8,128)(2,1)} %diag.3) | copy-start | bytes 1769476
  0.7 15.8 %copy-start.1 = (bf16[2,384,384]{2,1,0:T(8,128)(2,1)S(1)}, bf16[2,384,384]{2,1,0:T(8,128)(2,1)}, u32[]{:S(2)}) copy-start(bf16[2,384,384]{2,1,0:T(8,128)(2,1)} %precond.3) | copy-start | bytes 1769476
  0.7 15.8 %copy-start.5 = (f32[2,384]{1,0:T(2,128)S(1)}, f32[2,384]{1,0:T(2,128)}, u32[]{:S(2)}) copy-start(f32[2,384]{1,0:T(2,128)} %source.3) | copy-start | bytes 9220
  3.3 12.6 %collective-permute-start = (f32[2,384]{1,0:T(2,128)S(1)}, f32[2,384]{1,0:T(2,128)S(1)}, u32[]{:S(2)}, u32[]{:S(2)}) collective-permute-start(f32[2,384]{1,0:T(2,128)S(1)} %get-tuple-element.15), channel_id=1, source_target_pairs={{0,252},{1,253},{2,254},{3,255},{4,8},{5,9},{6,10},{7,11},{8,4},{9... | collective-permute-start | bytes 9224 | tf_op jit(solution)/shard_map/ppermute | solution.py:213
  6.1 9.9 %collective-permute-start.1 = (f32[2,384]{1,0:T(2,128)S(1)}, f32[2,384]{1,0:T(2,128)S(1)}, u32[]{:S(2)}, u32[]{:S(2)}) collective-permute-start(f32[2,384]{1,0:T(2,128)S(1)} %get-tuple-element.16), channel_id=1, source_target_pairs={{0,3},{1,2},{2,1},{3,0},{4,7},{5,6},{6,5},{7,4},{8,11},{9,10},{10,... | collective-permute-start | bytes 9224 | tf_op jit(solution)/shard_map/ppermute | solution.py:213
  8.6 7.4 %collective-permute-start.2 = (f32[2,384]{1,0:T(2,128)S(1)}, f32[2,384]{1,0:T(2,128)S(1)}, u32[]{:S(2)}, u32[]{:S(2)}) collective-permute-start(f32[2,384]{1,0:T(2,128)S(1)} %get-tuple-element.17), channel_id=1, source_target_pairs={{0,1},{1,0},{2,3},{3,2},{4,5},{5,4},{6,7},{7,6},{8,9},{9,8},{10,11... | collective-permute-start | bytes 9224 | tf_op jit(solution)/shard_map/ppermute | solution.py:213
  8.6 7.9 %collective-permute-start.3 = (f32[2,384]{1,0:T(2,128)S(1)}, f32[2,384]{1,0:T(2,128)S(1)}, u32[]{:S(2)}, u32[]{:S(2)}) collective-permute-start(f32[2,384]{1,0:T(2,128)S(1)} %get-tuple-element.18), channel_id=1, source_target_pairs={{0,4},{1,5},{2,6},{3,7},{4,0},{5,1},{6,2},{7,3},{8,12},{9,13},{10,... | collective-permute-start | bytes 9224 | tf_op jit(solution)/shard_map/ppermute | solution.py:213
  15.9 8.3 %copy-start.2 = (bf16[384,384]{1,0:T(8,128)(2,1)S(1)}, bf16[384,384]{1,0:T(8,128)(2,1)}, u32[]{:S(2)}) copy-start(bf16[384,384]{1,0:T(8,128)(2,1)} %surf.1) | copy-start | bytes 884740
  15.9 8.3 %copy-start.7 = (s32[2]{0:T(128)S(1)}, s32[2]{0:T(128)}, u32[]{:S(2)}) copy-start(s32[2]{0:T(128)} %param.16) | copy-start | bytes 28
  17.1 29.0 %copy-start.6 = (f32[1,384]{1,0:T(1,128)S(1)}, f32[1,384]{1,0:T(1,128)}, u32[]{:S(2)}) copy-start(f32[1,384]{1,0:T(1,128)} %grad.1) | copy-start | bytes 4612
  17.1 6.5 %collective-permute-start.4 = (f32[2,384]{1,0:T(2,128)S(1)}, f32[2,384]{1,0:T(2,128)S(1)}, u32[]{:S(2)}, u32[]{:S(2)}) collective-permute-start(f32[2,384]{1,0:T(2,128)S(1)} %get-tuple-element.20), channel_id=1, source_target_pairs={{0,252},{1,253},{2,254},{3,255},{4,8},{5,9},{6,10},{7,11},{8,4},{9... | collective-permute-start | bytes 9224 | tf_op jit(solution)/shard_map/ppermute | solution.py:213
  17.2 6.4 %collective-permute-start.5 = (f32[2,384]{1,0:T(2,128)S(1)}, f32[2,384]{1,0:T(2,128)S(1)}, u32[]{:S(2)}, u32[]{:S(2)}) collective-permute-start(f32[2,384]{1,0:T(2,128)S(1)} %get-tuple-element.21), channel_id=1, source_target_pairs={{0,1},{1,0},{2,3},{3,2},{4,5},{5,4},{6,7},{7,6},{8,9},{9,8},{10,11... | collective-permute-start | bytes 9224 | tf_op jit(solution)/shard_map/ppermute | solution.py:213
  18.8 4.8 %collective-permute-start.6 = (f32[2,384]{1,0:T(2,128)S(1)}, f32[2,384]{1,0:T(2,128)S(1)}, u32[]{:S(2)}, u32[]{:S(2)}) collective-permute-start(f32[2,384]{1,0:T(2,128)S(1)} %get-tuple-element.22), channel_id=1, source_target_pairs={{0,3},{1,2},{2,1},{3,0},{4,7},{5,6},{6,5},{7,4},{8,11},{9,10},{10,... | collective-permute-start | bytes 9224 | tf_op jit(solution)/shard_map/ppermute | solution.py:213
  19.0 5.2 %collective-permute-start.7 = (f32[2,384]{1,0:T(2,128)S(1)}, f32[2,384]{1,0:T(2,128)S(1)}, u32[]{:S(2)}, u32[]{:S(2)}) collective-permute-start(f32[2,384]{1,0:T(2,128)S(1)} %get-tuple-element.23), channel_id=1, source_target_pairs={{0,4},{1,5},{2,6},{3,7},{4,0},{5,1},{6,2},{7,3},{8,12},{9,13},{10,... | collective-permute-start | bytes 9224 | tf_op jit(solution)/shard_map/ppermute | solution.py:213

commit v6 on v5

--- a/solution.py
+++ b/solution.py
@@ -71,7 +71,7 @@
         out[...] = total
 
 
-def first_kernel(names_in, adjoint_in, off_in, c0, c1, c2, c3, off, names, adjoint, left, sums, sems):
+def first_kernel(names_in, adjoint_in, off_in, c0, c1, c2, c3, off, names, adjoint, sems):
     slots = [jnp.where(which == 0, even, odd) for even, odd, which in message_slots(0)]
     count = adjoint.shape[0]
     heads = [
@@ -80,36 +80,29 @@
     ]
 
     def block(m):
-        slot = sum(jnp.where(m == i, slots[i], 0) for i in range(len(slots)))
+        slot = (slots + [0])[m]
         return slot, pltpu.make_async_copy(off_in.at[:, slot], off.at[:, slot], sems.at[m])
 
     for copy in heads:
         copy.start()
 
-    @pl.loop(0, len(slots) + 1)
-    def _(m):
+    for m in range(len(slots) + 1):
         block(m)[1].start()
 
     for copy in heads:
         copy.wait()
+    left = {}
     for m, (even, odd, which) in enumerate(message_slots(0)):
         for row in range(count):
             here = slice(row, row + 1)
             name = jnp.where(which == 0, names[here, even : even + 1], names[here, odd : odd + 1])
             left[m, row] = placed(adjoint[here, :], count, name % count)
 
-    @pl.loop(0, len(slots))
-    def _(m):
+    for m, out in enumerate((c0, c1, c2, c3)):
         slot, copy = block(m)
         copy.wait()
-        sums[m] = jnp.zeros(sums.shape[1:], F32)
-
-        @pl.loop(0, count)
-        def _(row):
-            sums[m] += matmul(left[m, row], off[row, slot])
-
-    for m, out in enumerate((c0, c1, c2, c3)):
-        out[...] = sums[m]
+        parts = [matmul(left[m, row], off[row, slot]) for row in range(count)]
+        out[...] = sum(parts[1:], parts[0])
     block(len(slots))[1].wait()
 
 
@@ -201,6 +194,17 @@
     )
 
 
+LINE = [(0, 7), (0, 6), (0, 5), (0, 4), (0, 3), (0, 2), (0, 1), (0, 0), (1, 7), (1, 6), (1, 5), (1, 4), (1, 3), (1, 2), (1, 1), (1, 0)]
+
+
+def lines():
+    return [
+        [z * stride("z") + core * stride("core") + y * stride("y") + x for core, z in LINE]
+        for y in range(CUT["y"])
+        for x in range(CUT["x"])
+    ]
+
+
 def on_device(
     adjoint_start, source, jac_off, jac_diag, precond, surf_map, neighbours, owner, surface_grad
 ):
@@ -223,11 +227,9 @@
         [
             pltpu.VMEM(neighbours.shape, jnp.int32),
             pltpu.VMEM((count, width), F32),
-            pltpu.VMEM((4, count, count, width), BF16),
-            pltpu.VMEM((4, count, width), F32),
             pltpu.SemaphoreType.DMA((7,)),
         ],
-        52,
+        60,
     )(neighbours, adjoint_start, jac_off)
     came = swap(messages, 0)
     local_call = call(local_kernel, [VMEM] * 4, [block], "local", 8 * matrix, 8 * matrix)
@@ -248,7 +250,7 @@
         6 * matrix,
         6 * matrix,
     )(owner.reshape(1, count), adjoint, source, local, *came, precond, surf_map)
-    got = lax.all_to_all(payload, FIRST, 0, 0, tiled=True)
+    got = lax.all_to_all(payload, ALL, 0, 0, axis_index_groups=lines(), tiled=True)
     (sums,) = call(
         spread_kernel, [VMEM], [jax.ShapeDtypeStruct((line, 8, LANES), F32)], "spread"
     )(got)

time: 46.9 us -> 46.1 us (0.983)
  Pallas kernels: 5.03 us -> 4.5 us
    all_to_all x1, blocking collectives: 12.2 us -> 11.6 us  [on_device(): lax.all_to_all(payload, ALL, 0, 0, axis_index_groups=lines(), tiled=True)]
    pallas_call x1, Pallas kernels: 2.63 us -> 2.1 us  [on_device(): call(first_kernel, [HBM] * 3, [pltpu.VMEM((count, width), F32)] * 4 + [pl...]
where the time goes in v6:
time: 46.1 us; the launch traced here: 45.9 us
  blocking collectives  21 us (46%)
  starting transfers between devices  18.5 us (40%)
  Pallas kernels  4.5 us (10%)
  waiting for transfers between devices  1.02 us (2%)
  between operations  0.76 us (2%)
    ppermute x8, starting transfers between devices, swap(): lax.ppermute(m, ALL, route)  18.5 us
    all_to_all x1, blocking collectives, on_device(): lax.all_to_all(payload, ALL, 0, 0, axis_index_groups=lines(), tiled=True)  11.6 us
    all_to_all x1, blocking collectives, on_device(): parts = lax.all_to_all(sums, SECOND, 0, 0, tiled=True)  9.45 us
    pallas_call x1, Pallas kernels, on_device(): call(first_kernel, [HBM] * 3, [pltpu.VMEM((count, width), F32)] * 4 + [pl...  2.1 us
    ppermute x8, waiting for transfers between devices, swap(): lax.ppermute(m, ALL, route)  1.02 us
  transfers between devices with their start and end apart: 8, of which 2 were waited for; matrix products, arithmetic and copies ran while one was open for 0% of the time, Pallas kernels for 1%

profile of v6, /device:TPU:1, one launch (start us, length us, event | category | flops | bytes accessed | tf_op | source)
XLA Modules:
  0.0 45.9 jit_solution(7637116309538226886)
XLA Ops:
  0.7 2.1 %first.1 = (f32[2,384]{1,0:T(2,128)S(1)}, f32[2,384]{1,0:T(2,128)S(1)}, f32[2,384]{1,0:T(2,128)S(1)}, f32[2,384]{1,0:T(2,128)S(1)}, bf16[2,5,384,384]{3,2,1,0:T(8,128)(2,1)S(1)}) custom-call(s32[2,5]{1,0:T(2,128)} %names.5, f32[2,384]{1,0:T(2,128)} %adjoint.3, bf16[2,5,384,384]{3,2,1,0:T(8,128)(2,1)} %off_in.1), custom_call_target="tpu_custom_call" | custom-call | flops 2359296 | bytes 2359296 | tf_op jit(solution)/shard_map/first/pallas_call | solution.py:220
  2.8 0.0 copy-start.1
  2.8 2.8 %collective-permute-start = (f32[2,384]{1,0:T(2,128)S(1)}, f32[2,384]{1,0:T(2,128)S(1)}, u32[]{:S(2)}, u32[]{:S(2)}) collective-permute-start(f32[2,384]{1,0:T(2,128)S(1)} %get-tuple-element.15), channel_id=1, source_target_pairs={{0,252},{1,253},{2,254},{3,255},{4,8},{5,9},{6,10},{7,11},{8,4},{9... | collective-permute-start | bytes 9224 | tf_op jit(solution)/shard_map/ppermute | solution.py:217
  5.6 2.5 %collective-permute-start.1 = (f32[2,384]{1,0:T(2,128)S(1)}, f32[2,384]{1,0:T(2,128)S(1)}, u32[]{:S(2)}, u32[]{:S(2)}) collective-permute-start(f32[2,384]{1,0:T(2,128)S(1)} %get-tuple-element.16), channel_id=1, source_target_pairs={{0,3},{1,2},{2,1},{3,0},{4,7},{5,6},{6,5},{7,4},{8,11},{9,10},{10,... | collective-permute-start | bytes 9224 | tf_op jit(solution)/shard_map/ppermute | solution.py:217
  8.0 0.0 collective-permute-start.2
  8.0 7.1 %collective-permute-start.3 = (f32[2,384]{1,0:T(2,128)S(1)}, f32[2,384]{1,0:T(2,128)S(1)}, u32[]{:S(2)}, u32[]{:S(2)}) collective-permute-start(f32[2,384]{1,0:T(2,128)S(1)} %get-tuple-element.18), channel_id=1, source_target_pairs={{0,4},{1,5},{2,6},{3,7},{4,0},{5,1},{6,2},{7,3},{8,12},{9,13},{10,... | collective-permute-start | bytes 9224 | tf_op jit(solution)/shard_map/ppermute | solution.py:217
  15.1 0.3 local.2
  15.4 0.0 collective-permute-done.c0
  15.4 0.0 collective-permute-done.1.c1
  15.5 0.5 %collective-permute-done.3.c3 = f32[2,384]{1,0:T(2,128)S(1)} collective-permute-done((f32[2,384]{1,0:T(2,128)S(1)}, f32[2,384]{1,0:T(2,128)S(1)}, u32[]{:S(2)}, u32[]{:S(2)}) %collective-permute-start.3) | collective-permute-done | bytes 3104 | tf_op jit(solution)/shard_map/ppermute | solution.py:217
  15.9 0.7 %middle.1 = (f32[2,384]{1,0:T(2,128)S(1)}, f32[2,384]{1,0:T(2,128)S(1)}, f32[2,384]{1,0:T(2,128)S(1)}, f32[2,384]{1,0:T(2,128)S(1)}, f32[2,384]{1,0:T(2,128)S(1)}) custom-call(s32[2,5]{1,0:T(2,128)S(1)} %copy-done.4, f32[2,384]{1,0:T(2,128)S(1)} %copy-done.3, f32[2,384]{1,0:T(2,128)S(1)} %copy-done.5, f32[2,384]{1,0:T(2,128)S(1)} %local.2, ...), custom_call_target="tpu_custom_call" | custom-call | flops 2949120 | bytes 2949120 | tf_op jit(solution)/shard_map/middle/pallas_call | solution.py:237
  16.6 0.1 collective-permute-start.4
  16.7 1.6 %collective-permute-start.5 = (f32[2,384]{1,0:T(2,128)S(1)}, f32[2,384]{1,0:T(2,128)S(1)}, u32[]{:S(2)}, u32[]{:S(2)}) collective-permute-start(f32[2,384]{1,0:T(2,128)S(1)} %get-tuple-element.21), channel_id=1, source_target_pairs={{0,1},{1,0},{2,3},{3,2},{4,5},{5,4},{6,7},{7,6},{8,9},{9,8},{10,11... | collective-permute-start | bytes 9224 | tf_op jit(solution)/shard_map/ppermute | solution.py:217
  18.3 0.2 collective-permute-start.6
  18.5 4.3 %collective-permute-start.7 = (f32[2,384]{1,0:T(2,128)S(1)}, f32[2,384]{1,0:T(2,128)S(1)}, u32[]{:S(2)}, u32[]{:S(2)}) collective-permute-start(f32[2,384]{1,0:T(2,128)S(1)} %get-tuple-element.23), channel_id=1, source_target_pairs={{0,4},{1,5},{2,6},{3,7},{4,0},{5,1},{6,2},{7,3},{8,12},{9,13},{10,... | collective-permute-start | bytes 9224 | tf_op jit(solution)/shard_map/ppermute | solution.py:217
  22.8 0.3 local.3
  23.1 0.0 collective-permute-done.4.c0
  23.1 0.0 collective-permute-done.5.c1
  23.2 0.5 %collective-permute-done.7.c3 = f32[2,384]{1,0:T(2,128)S(1)} collective-permute-done((f32[2,384]{1,0:T(2,128)S(1)}, f32[2,384]{1,0:T(2,128)S(1)}, u32[]{:S(2)}, u32[]{:S(2)}) %collective-permute-start.7) | collective-permute-done | bytes 3104 | tf_op jit(solution)/shard_map/ppermute | solution.py:217
  23.7 0.3 last.1
  24.0 11.6 %all_to_all.10.got = f32[16,8,128]{2,1,0:T(8,128)S(1)} all-to-all(f32[16,8,128]{2,1,0:T(8,128)S(1)} %get-tuple-element.24), channel_id=1, replica_groups={{224,192,160,128,96,64,32,0,228,196,164,132,100,68,36,4},{225,193,161,1..., dimensions={0} | all-to-all | bytes 131072 | tf_op jit(solution)/shard_map/all_to_all | solution.py:253
  35.6 0.2 spread.1
  35.9 9.5 %all_to_all.11.parts = f32[16,8,128]{2,1,0:T(8,128)S(1)} all-to-all(f32[16,8,128]{2,1,0:T(8,128)S(1)} %spread.1), channel_id=1, replica_groups=mesh['z'=8,'y'=4,'core'=2,'x'=4] {'y','x'}, dimensions={0} | all-to-all | bytes 131072 | tf_op jit(solution)/shard_map/all_to_all | solution.py:257
  45.3 0.6 %finish.1 = (f32[2,384]{1,0:T(2,128)}, f32[1,384]{1,0:T(1,128)}) custom-call(f32[1,384]{1,0:T(1,128)S(1)} %copy-done.6, f32[16,8,128]{2,1,0:T(8,128)S(1)} %all_to_all.11.parts, f32[2,384]{1,0:T(2,128)S(1)} %get-tuple-element.25.values), custom_call_target="tpu_custom_call" | custom-call | tf_op jit(solution)/shard_map/finish/pallas_call | solution.py:258
  (17 shorter events, 0.0 us)
Async XLA Ops:
  0.6 14.5 %copy-start.4 = (s32[2,5]{1,0:T(2,128)S(1)}, s32[2,5]{1,0:T(2,128)}, u32[]{:S(2)}) copy-start(s32[2,5]{1,0:T(2,128)} %names.5) | copy-start | bytes 124
  0.6 14.5 %copy-start.3 = (f32[2,384]{1,0:T(2,128)S(1)}, f32[2,384]{1,0:T(2,128)}, u32[]{:S(2)}) copy-start(f32[2,384]{1,0:T(2,128)} %adjoint.3) | copy-start | bytes 9220
  0.7 14.5 %copy-start = (bf16[2,384,384]{2,1,0:T(8,128)(2,1)S(1)}, bf16[2,384,384]{2,1,0:T(8,128)(2,1)}, u32[]{:S(2)}) copy-start(bf16[2,384,384]{2,1,0:T(8,128)(2,1)} %diag.3) | copy-start | bytes 1769476
  0.7 15.3 %copy-start.5 = (f32[2,384]{1,0:T(2,128)S(1)}, f32[2,384]{1,0:T(2,128)}, u32[]{:S(2)}) copy-start(f32[2,384]{1,0:T(2,128)} %source.3) | copy-start | bytes 9220
  2.8 13.2 %copy-start.1 = (bf16[2,384,384]{2,1,0:T(8,128)(2,1)S(1)}, bf16[2,384,384]{2,1,0:T(8,128)(2,1)}, u32[]{:S(2)}) copy-start(bf16[2,384,384]{2,1,0:T(8,128)(2,1)} %precond.3) | copy-start | bytes 1769476
  2.8 12.6 %collective-permute-start = (f32[2,384]{1,0:T(2,128)S(1)}, f32[2,384]{1,0:T(2,128)S(1)}, u32[]{:S(2)}, u32[]{:S(2)}) collective-permute-start(f32[2,384]{1,0:T(2,128)S(1)} %get-tuple-element.15), channel_id=1, source_target_pairs={{0,252},{1,253},{2,254},{3,255},{4,8},{5,9},{6,10},{7,11},{8,4},{9... | collective-permute-start | bytes 9224 | tf_op jit(solution)/shard_map/ppermute | solution.py:217
  5.6 9.9 %collective-permute-start.1 = (f32[2,384]{1,0:T(2,128)S(1)}, f32[2,384]{1,0:T(2,128)S(1)}, u32[]{:S(2)}, u32[]{:S(2)}) collective-permute-start(f32[2,384]{1,0:T(2,128)S(1)} %get-tuple-element.16), channel_id=1, source_target_pairs={{0,3},{1,2},{2,1},{3,0},{4,7},{5,6},{6,5},{7,4},{8,11},{9,10},{10,... | collective-permute-start | bytes 9224 | tf_op jit(solution)/shard_map/ppermute | solution.py:217
  8.0 7.4 %collective-permute-start.2 = (f32[2,384]{1,0:T(2,128)S(1)}, f32[2,384]{1,0:T(2,128)S(1)}, u32[]{:S(2)}, u32[]{:S(2)}) collective-permute-start(f32[2,384]{1,0:T(2,128)S(1)} %get-tuple-element.17), channel_id=1, source_target_pairs={{0,1},{1,0},{2,3},{3,2},{4,5},{5,4},{6,7},{7,6},{8,9},{9,8},{10,11... | collective-permute-start | bytes 9224 | tf_op jit(solution)/shard_map/ppermute | solution.py:217
  8.0 7.9 %collective-permute-start.3 = (f32[2,384]{1,0:T(2,128)S(1)}, f32[2,384]{1,0:T(2,128)S(1)}, u32[]{:S(2)}, u32[]{:S(2)}) collective-permute-start(f32[2,384]{1,0:T(2,128)S(1)} %get-tuple-element.18), channel_id=1, source_target_pairs={{0,4},{1,5},{2,6},{3,7},{4,0},{5,1},{6,2},{7,3},{8,12},{9,13},{10,... | collective-permute-start | bytes 9224 | tf_op jit(solution)/shard_map/ppermute | solution.py:217
  15.4 8.3 %copy-start.2 = (bf16[384,384]{1,0:T(8,128)(2,1)S(1)}, bf16[384,384]{1,0:T(8,128)(2,1)}, u32[]{:S(2)}) copy-start(bf16[384,384]{1,0:T(8,128)(2,1)} %surf.1) | copy-start | bytes 884740
  15.4 8.3 %copy-start.7 = (s32[2]{0:T(128)S(1)}, s32[2]{0:T(128)}, u32[]{:S(2)}) copy-start(s32[2]{0:T(128)} %param.16) | copy-start | bytes 28
  16.6 28.7 %copy-start.6 = (f32[1,384]{1,0:T(1,128)S(1)}, f32[1,384]{1,0:T(1,128)}, u32[]{:S(2)}) copy-start(f32[1,384]{1,0:T(1,128)} %grad.1) | copy-start | bytes 4612
  16.6 6.5 %collective-permute-start.4 = (f32[2,384]{1,0:T(2,128)S(1)}, f32[2,384]{1,0:T(2,128)S(1)}, u32[]{:S(2)}, u32[]{:S(2)}) collective-permute-start(f32[2,384]{1,0:T(2,128)S(1)} %get-tuple-element.20), channel_id=1, source_target_pairs={{0,252},{1,253},{2,254},{3,255},{4,8},{5,9},{6,10},{7,11},{8,4},{9... | collective-permute-start | bytes 9224 | tf_op jit(solution)/shard_map/ppermute | solution.py:217
  16.7 6.4 %collective-permute-start.5 = (f32[2,384]{1,0:T(2,128)S(1)}, f32[2,384]{1,0:T(2,128)S(1)}, u32[]{:S(2)}, u32[]{:S(2)}) collective-permute-start(f32[2,384]{1,0:T(2,128)S(1)} %get-tuple-element.21), channel_id=1, source_target_pairs={{0,1},{1,0},{2,3},{3,2},{4,5},{5,4},{6,7},{7,6},{8,9},{9,8},{10,11... | collective-permute-start | bytes 9224 | tf_op jit(solution)/shard_map/ppermute | solution.py:217
  18.3 4.8 %collective-permute-start.6 = (f32[2,384]{1,0:T(2,128)S(1)}, f32[2,384]{1,0:T(2,128)S(1)}, u32[]{:S(2)}, u32[]{:S(2)}) collective-permute-start(f32[2,384]{1,0:T(2,128)S(1)} %get-tuple-element.22), channel_id=1, source_target_pairs={{0,3},{1,2},{2,1},{3,0},{4,7},{5,6},{6,5},{7,4},{8,11},{9,10},{10,... | collective-permute-start | bytes 9224 | tf_op jit(solution)/shard_map/ppermute | solution.py:217
  18.5 5.2 %collective-permute-start.7 = (f32[2,384]{1,0:T(2,128)S(1)}, f32[2,384]{1,0:T(2,128)S(1)}, u32[]{:S(2)}, u32[]{:S(2)}) collective-permute-start(f32[2,384]{1,0:T(2,128)S(1)} %get-tuple-element.23), channel_id=1, source_target_pairs={{0,4},{1,5},{2,6},{3,7},{4,0},{5,1},{6,2},{7,3},{8,12},{9,13},{10,... | collective-permute-start | bytes 9224 | tf_op jit(solution)/shard_map/ppermute | solution.py:217

commit v7 on v6

--- a/solution.py
+++ b/solution.py
@@ -155,11 +155,11 @@
     lanes = (got.shape[1] - 2) // 2
     lane = lax.broadcasted_iota(jnp.int32, (peers, LANES), 1)
     patch = sum(lax.axis_index(axis) * stride(axis) for axis in FIRST)
-    place = lane
+    group = out.shape[0]
+    place = jnp.maximum(group - 1 - lane, 0)
     for axis in reversed(SECOND):
         patch = patch + place % CUT[axis] * stride(axis)
         place = place // CUT[axis]
-    group = out.shape[0]
     patch = jnp.where(lane < group, patch, -1).astype(F32)
     hot = jnp.concatenate(
         [jnp.where(got[:, 2 * lanes + row, :] == patch, 1.0, 0.0).astype(BF16) for row in range(2)],
@@ -194,7 +194,7 @@
     )
 
 
-LINE = [(0, 7), (0, 6), (0, 5), (0, 4), (0, 3), (0, 2), (0, 1), (0, 0), (1, 7), (1, 6), (1, 5), (1, 4), (1, 3), (1, 2), (1, 1), (1, 0)]
+LINE = [(1, 7), (1, 6), (1, 5), (1, 4), (1, 3), (1, 2), (1, 1), (1, 0), (0, 7), (0, 6), (0, 5), (0, 4), (0, 3), (0, 2), (0, 1), (0, 0)]
 
 
 def lines():
@@ -202,6 +202,18 @@
         [z * stride("z") + core * stride("core") + y * stride("y") + x for core, z in LINE]
         for y in range(CUT["y"])
         for x in range(CUT["x"])
+    ]
+
+
+def planes():
+    return [
+        [
+            z * stride("z") + core * stride("core") + y * stride("y") + x
+            for y in reversed(range(CUT["y"]))
+            for x in reversed(range(CUT["x"]))
+        ]
+        for z in range(CUT["z"])
+        for core in range(CUT["core"])
     ]
 
 
@@ -254,7 +266,7 @@
     (sums,) = call(
         spread_kernel, [VMEM], [jax.ShapeDtypeStruct((line, 8, LANES), F32)], "spread"
     )(got)
-    parts = lax.all_to_all(sums, SECOND, 0, 0, tiled=True)
+    parts = lax.all_to_all(sums, ALL, 0, 0, axis_index_groups=planes(), tiled=True)
     adjoint, sensitivity = call(
         finish_kernel,
         [VMEM] * 3,

time: 46.1 us -> 45.4 us (0.985)
  blocking collectives: 21 us -> 20.4 us
where the time goes in v7:
time: 45.4 us; the launch traced here: 45.2 us
  blocking collectives  20.4 us (45%)
  starting transfers between devices  18.5 us (41%)
  Pallas kernels  4.5 us (10%)
  waiting for transfers between devices  1.02 us (2%)
  between operations  0.76 us (2%)
    ppermute x8, starting transfers between devices, swap(): lax.ppermute(m, ALL, route)  18.5 us
    all_to_all x1, blocking collectives, on_device(): lax.all_to_all(payload, ALL, 0, 0, axis_index_groups=lines(), tiled=True)  11.2 us
    all_to_all x1, blocking collectives, on_device(): lax.all_to_all(sums, ALL, 0, 0, axis_index_groups=planes(), tiled=True)  9.19 us
    pallas_call x1, Pallas kernels, on_device(): call(first_kernel, [HBM] * 3, [pltpu.VMEM((count, width), F32)] * 4 + [pl...  2.1 us
    ppermute x8, waiting for transfers between devices, swap(): lax.ppermute(m, ALL, route)  1.02 us
  transfers between devices with their start and end apart: 8, of which 2 were waited for; matrix products, arithmetic and copies ran while one was open for 0% of the time, Pallas kernels for 1%

profile of v7, /device:TPU:1, one launch (start us, length us, event | category | flops | bytes accessed | tf_op | source)
XLA Modules:
  0.0 45.2 jit_solution(15784098930476806685)
XLA Ops:
  0.7 2.1 %first.1 = (f32[2,384]{1,0:T(2,128)S(1)}, f32[2,384]{1,0:T(2,128)S(1)}, f32[2,384]{1,0:T(2,128)S(1)}, f32[2,384]{1,0:T(2,128)S(1)}, bf16[2,5,384,384]{3,2,1,0:T(8,128)(2,1)S(1)}) custom-call(s32[2,5]{1,0:T(2,128)} %names.5, f32[2,384]{1,0:T(2,128)} %adjoint.3, bf16[2,5,384,384]{3,2,1,0:T(8,128)(2,1)} %off_in.1), custom_call_target="tpu_custom_call" | custom-call | flops 2359296 | bytes 2359296 | tf_op jit(solution)/shard_map/first/pallas_call | solution.py:232
  2.8 0.0 copy-start.1
  2.8 2.8 %collective-permute-start = (f32[2,384]{1,0:T(2,128)S(1)}, f32[2,384]{1,0:T(2,128)S(1)}, u32[]{:S(2)}, u32[]{:S(2)}) collective-permute-start(f32[2,384]{1,0:T(2,128)S(1)} %get-tuple-element.15), channel_id=1, source_target_pairs={{0,252},{1,253},{2,254},{3,255},{4,8},{5,9},{6,10},{7,11},{8,4},{9... | collective-permute-start | bytes 9224 | tf_op jit(solution)/shard_map/ppermute | solution.py:229
  5.6 2.5 %collective-permute-start.1 = (f32[2,384]{1,0:T(2,128)S(1)}, f32[2,384]{1,0:T(2,128)S(1)}, u32[]{:S(2)}, u32[]{:S(2)}) collective-permute-start(f32[2,384]{1,0:T(2,128)S(1)} %get-tuple-element.16), channel_id=1, source_target_pairs={{0,3},{1,2},{2,1},{3,0},{4,7},{5,6},{6,5},{7,4},{8,11},{9,10},{10,... | collective-permute-start | bytes 9224 | tf_op jit(solution)/shard_map/ppermute | solution.py:229
  8.0 0.0 collective-permute-start.2
  8.0 7.1 %collective-permute-start.3 = (f32[2,384]{1,0:T(2,128)S(1)}, f32[2,384]{1,0:T(2,128)S(1)}, u32[]{:S(2)}, u32[]{:S(2)}) collective-permute-start(f32[2,384]{1,0:T(2,128)S(1)} %get-tuple-element.18), channel_id=1, source_target_pairs={{0,4},{1,5},{2,6},{3,7},{4,0},{5,1},{6,2},{7,3},{8,12},{9,13},{10,... | collective-permute-start | bytes 9224 | tf_op jit(solution)/shard_map/ppermute | solution.py:229
  15.1 0.3 local.2
  15.4 0.0 collective-permute-done.c0
  15.4 0.0 collective-permute-done.1.c1
  15.4 0.0 collective-permute-done.2.c2
  15.5 0.5 %collective-permute-done.3.c3 = f32[2,384]{1,0:T(2,128)S(1)} collective-permute-done((f32[2,384]{1,0:T(2,128)S(1)}, f32[2,384]{1,0:T(2,128)S(1)}, u32[]{:S(2)}, u32[]{:S(2)}) %collective-permute-start.3) | collective-permute-done | bytes 3104 | tf_op jit(solution)/shard_map/ppermute | solution.py:229
  15.9 0.7 %middle.1 = (f32[2,384]{1,0:T(2,128)S(1)}, f32[2,384]{1,0:T(2,128)S(1)}, f32[2,384]{1,0:T(2,128)S(1)}, f32[2,384]{1,0:T(2,128)S(1)}, f32[2,384]{1,0:T(2,128)S(1)}) custom-call(s32[2,5]{1,0:T(2,128)S(1)} %copy-done.4, f32[2,384]{1,0:T(2,128)S(1)} %copy-done.3, f32[2,384]{1,0:T(2,128)S(1)} %copy-done.5, f32[2,384]{1,0:T(2,128)S(1)} %local.2, ...), custom_call_target="tpu_custom_call" | custom-call | flops 2949120 | bytes 2949120 | tf_op jit(solution)/shard_map/middle/pallas_call | solution.py:249
  16.6 0.1 collective-permute-start.4
  16.7 1.6 %collective-permute-start.5 = (f32[2,384]{1,0:T(2,128)S(1)}, f32[2,384]{1,0:T(2,128)S(1)}, u32[]{:S(2)}, u32[]{:S(2)}) collective-permute-start(f32[2,384]{1,0:T(2,128)S(1)} %get-tuple-element.21), channel_id=1, source_target_pairs={{0,1},{1,0},{2,3},{3,2},{4,5},{5,4},{6,7},{7,6},{8,9},{9,8},{10,11... | collective-permute-start | bytes 9224 | tf_op jit(solution)/shard_map/ppermute | solution.py:229
  18.3 0.2 collective-permute-start.6
  18.5 4.3 %collective-permute-start.7 = (f32[2,384]{1,0:T(2,128)S(1)}, f32[2,384]{1,0:T(2,128)S(1)}, u32[]{:S(2)}, u32[]{:S(2)}) collective-permute-start(f32[2,384]{1,0:T(2,128)S(1)} %get-tuple-element.23), channel_id=1, source_target_pairs={{0,4},{1,5},{2,6},{3,7},{4,0},{5,1},{6,2},{7,3},{8,12},{9,13},{10,... | collective-permute-start | bytes 9224 | tf_op jit(solution)/shard_map/ppermute | solution.py:229
  22.8 0.3 local.3
  23.1 0.0 collective-permute-done.5.c1
  23.2 0.5 %collective-permute-done.7.c3 = f32[2,384]{1,0:T(2,128)S(1)} collective-permute-done((f32[2,384]{1,0:T(2,128)S(1)}, f32[2,384]{1,0:T(2,128)S(1)}, u32[]{:S(2)}, u32[]{:S(2)}) %collective-permute-start.7) | collective-permute-done | bytes 3104 | tf_op jit(solution)/shard_map/ppermute | solution.py:229
  23.7 0.3 last.1
  24.0 11.2 %all_to_all.10.got = f32[16,8,128]{2,1,0:T(8,128)S(1)} all-to-all(f32[16,8,128]{2,1,0:T(8,128)S(1)} %get-tuple-element.24), channel_id=1, replica_groups={{228,196,164,132,100,68,36,4,224,192,160,128,96,64,32,0},{229,197,165,1..., dimensions={0} | all-to-all | bytes 131072 | tf_op jit(solution)/shard_map/all_to_all | solution.py:265
  35.2 0.2 spread.1
  35.4 9.2 %all_to_all.11.parts = f32[16,8,128]{2,1,0:T(8,128)S(1)} all-to-all(f32[16,8,128]{2,1,0:T(8,128)S(1)} %spread.1), channel_id=1, replica_groups={{27,26,25,24,19,18,17,16,11,10,9,8,3,2,1,0},{31,30,29,28,23,22,21,20,15..., dimensions={0} | all-to-all | bytes 131072 | tf_op jit(solution)/shard_map/all_to_all | solution.py:269
  44.6 0.6 %finish.1 = (f32[2,384]{1,0:T(2,128)}, f32[1,384]{1,0:T(1,128)}) custom-call(f32[1,384]{1,0:T(1,128)S(1)} %copy-done.6, f32[16,8,128]{2,1,0:T(8,128)S(1)} %all_to_all.11.parts, f32[2,384]{1,0:T(2,128)S(1)} %get-tuple-element.25.values), custom_call_target="tpu_custom_call" | custom-call | tf_op jit(solution)/shard_map/finish/pallas_call | solution.py:270
  (17 shorter events, 0.0 us)
Async XLA Ops:
  0.6 14.5 %copy-start.4 = (s32[2,5]{1,0:T(2,128)S(1)}, s32[2,5]{1,0:T(2,128)}, u32[]{:S(2)}) copy-start(s32[2,5]{1,0:T(2,128)} %names.5) | copy-start | bytes 124
  0.6 14.5 %copy-start.3 = (f32[2,384]{1,0:T(2,128)S(1)}, f32[2,384]{1,0:T(2,128)}, u32[]{:S(2)}) copy-start(f32[2,384]{1,0:T(2,128)} %adjoint.3) | copy-start | bytes 9220
  0.7 14.5 %copy-start = (bf16[2,384,384]{2,1,0:T(8,128)(2,1)S(1)}, bf16[2,384,384]{2,1,0:T(8,128)(2,1)}, u32[]{:S(2)}) copy-start(bf16[2,384,384]{2,1,0:T(8,128)(2,1)} %diag.3) | copy-start | bytes 1769476
  0.7 15.3 %copy-start.5 = (f32[2,384]{1,0:T(2,128)S(1)}, f32[2,384]{1,0:T(2,128)}, u32[]{:S(2)}) copy-start(f32[2,384]{1,0:T(2,128)} %source.3) | copy-start | bytes 9220
  2.8 13.2 %copy-start.1 = (bf16[2,384,384]{2,1,0:T(8,128)(2,1)S(1)}, bf16[2,384,384]{2,1,0:T(8,128)(2,1)}, u32[]{:S(2)}) copy-start(bf16[2,384,384]{2,1,0:T(8,128)(2,1)} %precond.3) | copy-start | bytes 1769476
  2.8 12.6 %collective-permute-start = (f32[2,384]{1,0:T(2,128)S(1)}, f32[2,384]{1,0:T(2,128)S(1)}, u32[]{:S(2)}, u32[]{:S(2)}) collective-permute-start(f32[2,384]{1,0:T(2,128)S(1)} %get-tuple-element.15), channel_id=1, source_target_pairs={{0,252},{1,253},{2,254},{3,255},{4,8},{5,9},{6,10},{7,11},{8,4},{9... | collective-permute-start | bytes 9224 | tf_op jit(solution)/shard_map/ppermute | solution.py:229
  5.6 9.9 %collective-permute-start.1 = (f32[2,384]{1,0:T(2,128)S(1)}, f32[2,384]{1,0:T(2,128)S(1)}, u32[]{:S(2)}, u32[]{:S(2)}) collective-permute-start(f32[2,384]{1,0:T(2,128)S(1)} %get-tuple-element.16), channel_id=1, source_target_pairs={{0,3},{1,2},{2,1},{3,0},{4,7},{5,6},{6,5},{7,4},{8,11},{9,10},{10,... | collective-permute-start | bytes 9224 | tf_op jit(solution)/shard_map/ppermute | solution.py:229
  8.0 7.4 %collective-permute-start.2 = (f32[2,384]{1,0:T(2,128)S(1)}, f32[2,384]{1,0:T(2,128)S(1)}, u32[]{:S(2)}, u32[]{:S(2)}) collective-permute-start(f32[2,384]{1,0:T(2,128)S(1)} %get-tuple-element.17), channel_id=1, source_target_pairs={{0,1},{1,0},{2,3},{3,2},{4,5},{5,4},{6,7},{7,6},{8,9},{9,8},{10,11... | collective-permute-start | bytes 9224 | tf_op jit(solution)/shard_map/ppermute | solution.py:229
  8.0 7.9 %collective-permute-start.3 = (f32[2,384]{1,0:T(2,128)S(1)}, f32[2,384]{1,0:T(2,128)S(1)}, u32[]{:S(2)}, u32[]{:S(2)}) collective-permute-start(f32[2,384]{1,0:T(2,128)S(1)} %get-tuple-element.18), channel_id=1, source_target_pairs={{0,4},{1,5},{2,6},{3,7},{4,0},{5,1},{6,2},{7,3},{8,12},{9,13},{10,... | collective-permute-start | bytes 9224 | tf_op jit(solution)/shard_map/ppermute | solution.py:229
  15.4 8.3 %copy-start.2 = (bf16[384,384]{1,0:T(8,128)(2,1)S(1)}, bf16[384,384]{1,0:T(8,128)(2,1)}, u32[]{:S(2)}) copy-start(bf16[384,384]{1,0:T(8,128)(2,1)} %surf.1) | copy-start | bytes 884740
  15.4 8.3 %copy-start.7 = (s32[2]{0:T(128)S(1)}, s32[2]{0:T(128)}, u32[]{:S(2)}) copy-start(s32[2]{0:T(128)} %param.16) | copy-start | bytes 28
  16.6 28.0 %copy-start.6 = (f32[1,384]{1,0:T(1,128)S(1)}, f32[1,384]{1,0:T(1,128)}, u32[]{:S(2)}) copy-start(f32[1,384]{1,0:T(1,128)} %grad.1) | copy-start | bytes 4612
  16.6 6.5 %collective-permute-start.4 = (f32[2,384]{1,0:T(2,128)S(1)}, f32[2,384]{1,0:T(2,128)S(1)}, u32[]{:S(2)}, u32[]{:S(2)}) collective-permute-start(f32[2,384]{1,0:T(2,128)S(1)} %get-tuple-element.20), channel_id=1, source_target_pairs={{0,252},{1,253},{2,254},{3,255},{4,8},{5,9},{6,10},{7,11},{8,4},{9... | collective-permute-start | bytes 9224 | tf_op jit(solution)/shard_map/ppermute | solution.py:229
  16.7 6.4 %collective-permute-start.5 = (f32[2,384]{1,0:T(2,128)S(1)}, f32[2,384]{1,0:T(2,128)S(1)}, u32[]{:S(2)}, u32[]{:S(2)}) collective-permute-start(f32[2,384]{1,0:T(2,128)S(1)} %get-tuple-element.21), channel_id=1, source_target_pairs={{0,1},{1,0},{2,3},{3,2},{4,5},{5,4},{6,7},{7,6},{8,9},{9,8},{10,11... | collective-permute-start | bytes 9224 | tf_op jit(solution)/shard_map/ppermute | solution.py:229
  18.3 4.8 %collective-permute-start.6 = (f32[2,384]{1,0:T(2,128)S(1)}, f32[2,384]{1,0:T(2,128)S(1)}, u32[]{:S(2)}, u32[]{:S(2)}) collective-permute-start(f32[2,384]{1,0:T(2,128)S(1)} %get-tuple-element.22), channel_id=1, source_target_pairs={{0,3},{1,2},{2,1},{3,0},{4,7},{5,6},{6,5},{7,4},{8,11},{9,10},{10,... | collective-permute-start | bytes 9224 | tf_op jit(solution)/shard_map/ppermute | solution.py:229
  18.5 5.2 %collective-permute-start.7 = (f32[2,384]{1,0:T(2,128)S(1)}, f32[2,384]{1,0:T(2,128)S(1)}, u32[]{:S(2)}, u32[]{:S(2)}) collective-permute-start(f32[2,384]{1,0:T(2,128)S(1)} %get-tuple-element.23), channel_id=1, source_target_pairs={{0,4},{1,5},{2,6},{3,7},{4,0},{5,1},{6,2},{7,3},{8,12},{9,13},{10,... | collective-permute-start | bytes 9224 | tf_op jit(solution)/shard_map/ppermute | solution.py:229

commit v8 on v7

--- a/solution.py
+++ b/solution.py
@@ -194,7 +194,7 @@
     )
 
 
-LINE = [(1, 7), (1, 6), (1, 5), (1, 4), (1, 3), (1, 2), (1, 1), (1, 0), (0, 7), (0, 6), (0, 5), (0, 4), (0, 3), (0, 2), (0, 1), (0, 0)]
+LINE = [(1, 7), (0, 7), (1, 6), (0, 6), (1, 5), (0, 5), (1, 4), (0, 4), (1, 3), (0, 3), (1, 2), (0, 2), (1, 1), (0, 1), (1, 0), (0, 0)]
 
 
 def lines():
@@ -264,7 +264,7 @@
     )(owner.reshape(1, count), adjoint, source, local, *came, precond, surf_map)
     got = lax.all_to_all(payload, ALL, 0, 0, axis_index_groups=lines(), tiled=True)
     (sums,) = call(
-        spread_kernel, [VMEM], [jax.ShapeDtypeStruct((line, 8, LANES), F32)], "spread"
+        spread_kernel, [VMEM], [jax.ShapeDtypeStruct((line, 4, LANES), F32)], "spread"
     )(got)
     parts = lax.all_to_all(sums, ALL, 0, 0, axis_index_groups=planes(), tiled=True)
     adjoint, sensitivity = call(

time: 45.4 us -> 45.2 us (level)
  no operation moved by 1% of the time
where the time goes in v8:
time: 45.2 us; the launch traced here: 45 us
  blocking collectives  20.2 us (45%)
  starting transfers between devices  18.5 us (41%)
  Pallas kernels  4.49 us (10%)
  waiting for transfers between devices  1.02 us (2%)
  between operations  0.76 us (2%)
    ppermute x8, starting transfers between devices, swap(): lax.ppermute(m, ALL, route)  18.5 us
    all_to_all x1, blocking collectives, on_device(): lax.all_to_all(payload, ALL, 0, 0, axis_index_groups=lines(), tiled=True)  11 us
    all_to_all x1, blocking collectives, on_device(): lax.all_to_all(sums, ALL, 0, 0, axis_index_groups=planes(), tiled=True)  9.15 us
    pallas_call x1, Pallas kernels, on_device(): call(first_kernel, [HBM] * 3, [pltpu.VMEM((count, width), F32)] * 4 + [pl...  2.1 us
    ppermute x8, waiting for transfers between devices, swap(): lax.ppermute(m, ALL, route)  1.02 us
  transfers between devices with their start and end apart: 8, of which 2 were waited for; matrix products, arithmetic and copies ran while one was open for 0% of the time, Pallas kernels for 1%

profile of v8, /device:TPU:1, one launch (start us, length us, event | category | flops | bytes accessed | tf_op | source)
XLA Modules:
  0.0 45.0 jit_solution(150887451711505861)
XLA Ops:
  0.7 2.1 %first.1 = (f32[2,384]{1,0:T(2,128)S(1)}, f32[2,384]{1,0:T(2,128)S(1)}, f32[2,384]{1,0:T(2,128)S(1)}, f32[2,384]{1,0:T(2,128)S(1)}, bf16[2,5,384,384]{3,2,1,0:T(8,128)(2,1)S(1)}) custom-call(s32[2,5]{1,0:T(2,128)} %names.5, f32[2,384]{1,0:T(2,128)} %adjoint.3, bf16[2,5,384,384]{3,2,1,0:T(8,128)(2,1)} %off_in.1), custom_call_target="tpu_custom_call" | custom-call | flops 2359296 | bytes 2359296 | tf_op jit(solution)/shard_map/first/pallas_call | solution.py:232
  2.8 0.0 copy-start.1
  2.8 2.8 %collective-permute-start = (f32[2,384]{1,0:T(2,128)S(1)}, f32[2,384]{1,0:T(2,128)S(1)}, u32[]{:S(2)}, u32[]{:S(2)}) collective-permute-start(f32[2,384]{1,0:T(2,128)S(1)} %get-tuple-element.15), channel_id=1, source_target_pairs={{0,252},{1,253},{2,254},{3,255},{4,8},{5,9},{6,10},{7,11},{8,4},{9... | collective-permute-start | bytes 9224 | tf_op jit(solution)/shard_map/ppermute | solution.py:229
  5.6 2.5 %collective-permute-start.1 = (f32[2,384]{1,0:T(2,128)S(1)}, f32[2,384]{1,0:T(2,128)S(1)}, u32[]{:S(2)}, u32[]{:S(2)}) collective-permute-start(f32[2,384]{1,0:T(2,128)S(1)} %get-tuple-element.16), channel_id=1, source_target_pairs={{0,3},{1,2},{2,1},{3,0},{4,7},{5,6},{6,5},{7,4},{8,11},{9,10},{10,... | collective-permute-start | bytes 9224 | tf_op jit(solution)/shard_map/ppermute | solution.py:229
  8.0 7.1 %collective-permute-start.3 = (f32[2,384]{1,0:T(2,128)S(1)}, f32[2,384]{1,0:T(2,128)S(1)}, u32[]{:S(2)}, u32[]{:S(2)}) collective-permute-start(f32[2,384]{1,0:T(2,128)S(1)} %get-tuple-element.18), channel_id=1, source_target_pairs={{0,4},{1,5},{2,6},{3,7},{4,0},{5,1},{6,2},{7,3},{8,12},{9,13},{10,... | collective-permute-start | bytes 9224 | tf_op jit(solution)/shard_map/ppermute | solution.py:229
  15.1 0.3 local.2
  15.4 0.0 collective-permute-done.c0
  15.4 0.0 collective-permute-done.1.c1
  15.4 0.0 collective-permute-done.2.c2
  15.5 0.5 %collective-permute-done.3.c3 = f32[2,384]{1,0:T(2,128)S(1)} collective-permute-done((f32[2,384]{1,0:T(2,128)S(1)}, f32[2,384]{1,0:T(2,128)S(1)}, u32[]{:S(2)}, u32[]{:S(2)}) %collective-permute-start.3) | collective-permute-done | bytes 3104 | tf_op jit(solution)/shard_map/ppermute | solution.py:229
  15.9 0.7 %middle.1 = (f32[2,384]{1,0:T(2,128)S(1)}, f32[2,384]{1,0:T(2,128)S(1)}, f32[2,384]{1,0:T(2,128)S(1)}, f32[2,384]{1,0:T(2,128)S(1)}, f32[2,384]{1,0:T(2,128)S(1)}) custom-call(s32[2,5]{1,0:T(2,128)S(1)} %copy-done.4, f32[2,384]{1,0:T(2,128)S(1)} %copy-done.3, f32[2,384]{1,0:T(2,128)S(1)} %copy-done.5, f32[2,384]{1,0:T(2,128)S(1)} %local.2, ...), custom_call_target="tpu_custom_call" | custom-call | flops 2949120 | bytes 2949120 | tf_op jit(solution)/shard_map/middle/pallas_call | solution.py:249
  16.6 0.1 collective-permute-start.4
  16.7 1.6 %collective-permute-start.5 = (f32[2,384]{1,0:T(2,128)S(1)}, f32[2,384]{1,0:T(2,128)S(1)}, u32[]{:S(2)}, u32[]{:S(2)}) collective-permute-start(f32[2,384]{1,0:T(2,128)S(1)} %get-tuple-element.21), channel_id=1, source_target_pairs={{0,1},{1,0},{2,3},{3,2},{4,5},{5,4},{6,7},{7,6},{8,9},{9,8},{10,11... | collective-permute-start | bytes 9224 | tf_op jit(solution)/shard_map/ppermute | solution.py:229
  18.3 0.2 collective-permute-start.6
  18.5 4.3 %collective-permute-start.7 = (f32[2,384]{1,0:T(2,128)S(1)}, f32[2,384]{1,0:T(2,128)S(1)}, u32[]{:S(2)}, u32[]{:S(2)}) collective-permute-start(f32[2,384]{1,0:T(2,128)S(1)} %get-tuple-element.23), channel_id=1, source_target_pairs={{0,4},{1,5},{2,6},{3,7},{4,0},{5,1},{6,2},{7,3},{8,12},{9,13},{10,... | collective-permute-start | bytes 9224 | tf_op jit(solution)/shard_map/ppermute | solution.py:229
  22.8 0.3 local.3
  23.1 0.0 collective-permute-done.4.c0
  23.1 0.0 collective-permute-done.5.c1
  23.2 0.5 %collective-permute-done.7.c3 = f32[2,384]{1,0:T(2,128)S(1)} collective-permute-done((f32[2,384]{1,0:T(2,128)S(1)}, f32[2,384]{1,0:T(2,128)S(1)}, u32[]{:S(2)}, u32[]{:S(2)}) %collective-permute-start.7) | collective-permute-done | bytes 3104 | tf_op jit(solution)/shard_map/ppermute | solution.py:229
  23.7 0.3 last.1
  24.0 11.0 %all_to_all.10.got = f32[16,8,128]{2,1,0:T(8,128)S(1)} all-to-all(f32[16,8,128]{2,1,0:T(8,128)S(1)} %get-tuple-element.24), channel_id=1, replica_groups={{228,224,196,192,164,160,132,128,100,96,68,64,36,32,4,0},{229,225,197,1..., dimensions={0} | all-to-all | bytes 131072 | tf_op jit(solution)/shard_map/all_to_all | solution.py:265
  35.1 0.2 spread.1
  35.3 9.1 %all_to_all.11.parts = f32[16,4,128]{2,1,0:T(4,128)S(1)} all-to-all(f32[16,4,128]{2,1,0:T(4,128)S(1)} %spread.1), channel_id=1, replica_groups={{27,26,25,24,19,18,17,16,11,10,9,8,3,2,1,0},{31,30,29,28,23,22,21,20,15..., dimensions={0} | all-to-all | bytes 65536 | tf_op jit(solution)/shard_map/all_to_all | solution.py:269
  44.5 0.6 %finish.1 = (f32[2,384]{1,0:T(2,128)}, f32[1,384]{1,0:T(1,128)}) custom-call(f32[1,384]{1,0:T(1,128)S(1)} %copy-done.6, f32[16,4,128]{2,1,0:T(4,128)S(1)} %all_to_all.11.parts, f32[2,384]{1,0:T(2,128)S(1)} %get-tuple-element.25.values), custom_call_target="tpu_custom_call" | custom-call | tf_op jit(solution)/shard_map/finish/pallas_call | solution.py:270
  (17 shorter events, 0.0 us)
Async XLA Ops:
  0.6 14.5 %copy-start.4 = (s32[2,5]{1,0:T(2,128)S(1)}, s32[2,5]{1,0:T(2,128)}, u32[]{:S(2)}) copy-start(s32[2,5]{1,0:T(2,128)} %names.5) | copy-start | bytes 124
  0.6 14.5 %copy-start.3 = (f32[2,384]{1,0:T(2,128)S(1)}, f32[2,384]{1,0:T(2,128)}, u32[]{:S(2)}) copy-start(f32[2,384]{1,0:T(2,128)} %adjoint.3) | copy-start | bytes 9220
  0.7 14.5 %copy-start = (bf16[2,384,384]{2,1,0:T(8,128)(2,1)S(1)}, bf16[2,384,384]{2,1,0:T(8,128)(2,1)}, u32[]{:S(2)}) copy-start(bf16[2,384,384]{2,1,0:T(8,128)(2,1)} %diag.3) | copy-start | bytes 1769476
  0.7 15.3 %copy-start.5 = (f32[2,384]{1,0:T(2,128)S(1)}, f32[2,384]{1,0:T(2,128)}, u32[]{:S(2)}) copy-start(f32[2,384]{1,0:T(2,128)} %source.3) | copy-start | bytes 9220
  2.8 13.2 %copy-start.1 = (bf16[2,384,384]{2,1,0:T(8,128)(2,1)S(1)}, bf16[2,384,384]{2,1,0:T(8,128)(2,1)}, u32[]{:S(2)}) copy-start(bf16[2,384,384]{2,1,0:T(8,128)(2,1)} %precond.3) | copy-start | bytes 1769476
  2.8 12.6 %collective-permute-start = (f32[2,384]{1,0:T(2,128)S(1)}, f32[2,384]{1,0:T(2,128)S(1)}, u32[]{:S(2)}, u32[]{:S(2)}) collective-permute-start(f32[2,384]{1,0:T(2,128)S(1)} %get-tuple-element.15), channel_id=1, source_target_pairs={{0,252},{1,253},{2,254},{3,255},{4,8},{5,9},{6,10},{7,11},{8,4},{9... | collective-permute-start | bytes 9224 | tf_op jit(solution)/shard_map/ppermute | solution.py:229
  5.6 9.9 %collective-permute-start.1 = (f32[2,384]{1,0:T(2,128)S(1)}, f32[2,384]{1,0:T(2,128)S(1)}, u32[]{:S(2)}, u32[]{:S(2)}) collective-permute-start(f32[2,384]{1,0:T(2,128)S(1)} %get-tuple-element.16), channel_id=1, source_target_pairs={{0,3},{1,2},{2,1},{3,0},{4,7},{5,6},{6,5},{7,4},{8,11},{9,10},{10,... | collective-permute-start | bytes 9224 | tf_op jit(solution)/shard_map/ppermute | solution.py:229
  8.0 7.4 %collective-permute-start.2 = (f32[2,384]{1,0:T(2,128)S(1)}, f32[2,384]{1,0:T(2,128)S(1)}, u32[]{:S(2)}, u32[]{:S(2)}) collective-permute-start(f32[2,384]{1,0:T(2,128)S(1)} %get-tuple-element.17), channel_id=1, source_target_pairs={{0,1},{1,0},{2,3},{3,2},{4,5},{5,4},{6,7},{7,6},{8,9},{9,8},{10,11... | collective-permute-start | bytes 9224 | tf_op jit(solution)/shard_map/ppermute | solution.py:229
  8.0 7.9 %collective-permute-start.3 = (f32[2,384]{1,0:T(2,128)S(1)}, f32[2,384]{1,0:T(2,128)S(1)}, u32[]{:S(2)}, u32[]{:S(2)}) collective-permute-start(f32[2,384]{1,0:T(2,128)S(1)} %get-tuple-element.18), channel_id=1, source_target_pairs={{0,4},{1,5},{2,6},{3,7},{4,0},{5,1},{6,2},{7,3},{8,12},{9,13},{10,... | collective-permute-start | bytes 9224 | tf_op jit(solution)/shard_map/ppermute | solution.py:229
  15.4 8.3 %copy-start.2 = (bf16[384,384]{1,0:T(8,128)(2,1)S(1)}, bf16[384,384]{1,0:T(8,128)(2,1)}, u32[]{:S(2)}) copy-start(bf16[384,384]{1,0:T(8,128)(2,1)} %surf.1) | copy-start | bytes 884740
  15.4 8.3 %copy-start.7 = (s32[2]{0:T(128)S(1)}, s32[2]{0:T(128)}, u32[]{:S(2)}) copy-start(s32[2]{0:T(128)} %param.16) | copy-start | bytes 28
  16.6 27.8 %copy-start.6 = (f32[1,384]{1,0:T(1,128)S(1)}, f32[1,384]{1,0:T(1,128)}, u32[]{:S(2)}) copy-start(f32[1,384]{1,0:T(1,128)} %grad.1) | copy-start | bytes 4612
  16.6 6.5 %collective-permute-start.4 = (f32[2,384]{1,0:T(2,128)S(1)}, f32[2,384]{1,0:T(2,128)S(1)}, u32[]{:S(2)}, u32[]{:S(2)}) collective-permute-start(f32[2,384]{1,0:T(2,128)S(1)} %get-tuple-element.20), channel_id=1, source_target_pairs={{0,252},{1,253},{2,254},{3,255},{4,8},{5,9},{6,10},{7,11},{8,4},{9... | collective-permute-start | bytes 9224 | tf_op jit(solution)/shard_map/ppermute | solution.py:229
  16.7 6.4 %collective-permute-start.5 = (f32[2,384]{1,0:T(2,128)S(1)}, f32[2,384]{1,0:T(2,128)S(1)}, u32[]{:S(2)}, u32[]{:S(2)}) collective-permute-start(f32[2,384]{1,0:T(2,128)S(1)} %get-tuple-element.21), channel_id=1, source_target_pairs={{0,1},{1,0},{2,3},{3,2},{4,5},{5,4},{6,7},{7,6},{8,9},{9,8},{10,11... | collective-permute-start | bytes 9224 | tf_op jit(solution)/shard_map/ppermute | solution.py:229
  18.3 4.8 %collective-permute-start.6 = (f32[2,384]{1,0:T(2,128)S(1)}, f32[2,384]{1,0:T(2,128)S(1)}, u32[]{:S(2)}, u32[]{:S(2)}) collective-permute-start(f32[2,384]{1,0:T(2,128)S(1)} %get-tuple-element.22), channel_id=1, source_target_pairs={{0,3},{1,2},{2,1},{3,0},{4,7},{5,6},{6,5},{7,4},{8,11},{9,10},{10,... | collective-permute-start | bytes 9224 | tf_op jit(solution)/shard_map/ppermute | solution.py:229
  18.5 5.2 %collective-permute-start.7 = (f32[2,384]{1,0:T(2,128)S(1)}, f32[2,384]{1,0:T(2,128)S(1)}, u32[]{:S(2)}, u32[]{:S(2)}) collective-permute-start(f32[2,384]{1,0:T(2,128)S(1)} %get-tuple-element.23), channel_id=1, source_target_pairs={{0,4},{1,5},{2,6},{3,7},{4,0},{5,1},{6,2},{7,3},{8,12},{9,13},{10,... | collective-permute-start | bytes 9224 | tf_op jit(solution)/shard_map/ppermute | solution.py:229
